TPU v7x, 512 devices: a whole 4x8x8 slice. The times are simulated.
512 devices in a mesh: dp: 32 (over y, x), tensor: 16 (over z, core).
Axes of the slice: x: 4, y: 8, z: 8, core: 2. Of those that a mesh axis runs over, the one named last changes fastest.
Arguments:
- hidden_acts: bfloat16 [8192, 53248], P('dp', 'tensor'), parts along dimension 0, may hold values from -6 to 6
- mixing: float32 [52, 52], replicated, may hold values from -0.875 to 0.875
- packed_codes: int32 [53248, 256], P('tensor'), may hold values from 0 to 65535, as said below
- exponents: int32 [1024], replicated, may hold values from -1 to 1
Outputs:
- projected: bfloat16 [8192, 1024], P('dp', 'tensor'), parts along dimension 0
There are 32 independent parts, one for each index of `dp`. A program takes and returns all parts, laid end to end along the dimension named above; an argument that names none is the same for every part. Nothing has to cross between parts.
Inputs may be any that keep to these rules, and one draw needn't show every extreme that they name: `packed_codes`: each word holds four independent 4-bit fields in its low 16 bits, each uniform over its 16 patterns; the higher bits are zero.
All inputs are finite; a program needn't handle non-finite values.
Results may differ from a plain program's by a relative error of at most 0.015.
Values may be sent and summed in bfloat16 or wider, within the bound.
A program may use at most 64 MiB of HBM per device.

v0:
```python
import jax
import jax.numpy as jnp
from jax import lax
from jax.sharding import PartitionSpec as P

OUTER = 16
INNER_H = 64
INNER_M = 52


def partner_2(block, axis, stride):
    count = lax.axis_size(axis)
    route = []
    for low in range(count):
        high = low | 1 << stride
        if high != low and high < count:
            route += [(low, high), (high, low)]
    return lax.ppermute(block, axis, route)


def sylvester(order):
    index = jnp.arange(order, dtype=jnp.int32)
    both = index[:, None] & index[None, :]
    parity = jnp.zeros((order, order), jnp.int32)
    for bit_pos in range(max(order.bit_length() - 1, 0)):
        parity = parity + (both >> bit_pos & 1)
    return (1 - 2 * (parity & 1)).astype(jnp.float32)


def per_device(hidden_acts, mixing, packed_codes, exponents):
    groups = lax.axis_size("tensor")
    rows = hidden_acts.shape[0]
    local_blocks = OUTER // groups
    width = INNER_H * INNER_M
    flat = hidden_acts.astype(jnp.float32).reshape(rows * local_blocks * INNER_H, INNER_M)
    mixed = jnp.dot(flat, mixing, precision=lax.Precision.HIGHEST).reshape(
        rows * local_blocks, INNER_H, INNER_M
    )
    inner = (
        jnp.einsum("xcg,cd->xdg", mixed, sylvester(INNER_H), precision=lax.Precision.HIGHEST) / 8.0
    )
    inner = inner.astype(jnp.bfloat16).reshape(rows, local_blocks, width)
    values = jnp.einsum(
        "rlb,lm->rmb",
        inner.astype(jnp.float32),
        sylvester(local_blocks),
        precision=lax.Precision.HIGHEST,
    )
    position = lax.axis_index("tensor")
    for bit_pos in range(groups.bit_length() - 1):
        partner = partner_2(values, "tensor", bit_pos)
        upper = position >> bit_pos & 1 == 1
        values = jnp.where(upper, partner - values, values + partner)
    rotated = (values / 4.0).astype(jnp.bfloat16)
    rotated = rotated.reshape(rows, local_blocks * width)
    pieces = []
    for k in range(4):
        field = jnp.right_shift(jnp.left_shift(packed_codes, 28 - 4 * k), 28)
        pieces.append(
            jnp.dot(rotated, field.astype(jnp.bfloat16), preferred_element_type=jnp.float32)
        )
    partial_sums = jnp.concatenate(pieces, axis=1)
    owned = lax.psum_scatter(partial_sums, "tensor", scatter_dimension=1, tiled=True)
    span = owned.shape[1]
    start = lax.axis_index("tensor") * span
    own_exponents = lax.dynamic_slice_in_dim(exponents, start, span, 0)
    scale = jnp.exp2(own_exponents.astype(jnp.float32)) / 1024.0
    return (owned * scale[None, :]).astype(jnp.bfloat16)


def solution(mesh):
    placed = (P("dp", "tensor"), P(), P("tensor", None), P())
    return jax.shard_map(
        per_device, mesh=mesh, in_specs=placed, out_specs=P("dp", "tensor"), check_vma=False
    )
```

profile of v0, /device:TPU:1, one launch (start us, length us, event | category | flops | bytes accessed | tf_op | source)
XLA Modules:
  0.0 505.2 jit_solution(5640610449325819836)
XLA Ops:
  6.5 0.0 copy-start
  6.5 0.0 reduce-scatter.2.cloned.1.call-start
  6.5 3.8 copy.5
  10.3 2.4 dot_general.23
  12.7 0.0 copy-done
  12.7 1.7 fusion.43
  14.5 4.1 convert_bitcast_fusion
  18.6 3.8 copy.6
  22.4 2.9 reshape.17
  25.2 0.0 copy-start.3
  25.2 8.8 %collective-permute-start = (f32[256,1,3328]{0,2,1:T(8,128)S(1)}, f32[256,1,3328]{0,2,1:T(8,128)}, u32[]{:S(2)}, u32[]{:S(2)}) collective-permute-start(f32[256,1,3328]{0,2,1:T(8,128)S(1)} %reshape.17), channel_id=1, source_target_pairs={{0,1},{1,0},{2,3},{3,2},{4,5},{5,4},{6,7},{7,6},{8,9},{9,8},{10,11... | collective-permute-start | bytes 10223624 | tf_op jit(solution)/shard_map/ppermute | solution.py:18
  34.0 5.8 %collective-permute-done = f32[256,1,3328]{0,2,1:T(8,128)} collective-permute-done((f32[256,1,3328]{0,2,1:T(8,128)S(1)}, f32[256,1,3328]{0,2,1:T(8,128)}, u32[]{:S(2)}, u32[]{:S(2)}) %collective-permute-start) | collective-permute-done | bytes 3407904 | tf_op jit(solution)/shard_map/ppermute | solution.py:18
  39.8 3.4 add_select_fusion.2
  43.3 1.9 collective-permute-start.1
  45.2 75.0 %collective-permute-done.1 = f32[256,1,3328]{0,2,1:T(8,128)} collective-permute-done((f32[256,1,3328]{0,2,1:T(8,128)S(1)}, f32[256,1,3328]{0,2,1:T(8,128)}, u32[]{:S(2)}, u32[]{:S(2)}) %collective-permute-start.1) | collective-permute-done | bytes 3407904 | tf_op jit(solution)/shard_map/ppermute | solution.py:18
  120.2 3.4 add_select_fusion.1
  123.6 1.9 collective-permute-start.2
  125.6 149.6 %collective-permute-done.2 = f32[256,1,3328]{0,2,1:T(8,128)} collective-permute-done((f32[256,1,3328]{0,2,1:T(8,128)S(1)}, f32[256,1,3328]{0,2,1:T(8,128)}, u32[]{:S(2)}, u32[]{:S(2)}) %collective-permute-start.2) | collective-permute-done | bytes 3407904 | tf_op jit(solution)/shard_map/ppermute | solution.py:18
  275.2 4.3 add_select_fusion
  279.5 4.5 collective-permute-start.3
  284.0 0.0 copy-start.1
  284.0 149.4 %collective-permute-done.3 = f32[256,1,3328]{0,2,1:T(8,128)S(1)} collective-permute-done((f32[256,1,3328]{0,2,1:T(8,128)}, f32[256,1,3328]{0,2,1:T(8,128)S(1)}, u32[]{:S(2)}, u32[]{:S(2)}) %collective-permute-start.3) | collective-permute-done | bytes 3407904 | tf_op jit(solution)/shard_map/ppermute | solution.py:18
  433.4 2.7 fusion.6
  436.1 0.8 fusion.10
  436.9 0.8 fusion.9
  437.8 0.8 fusion.8
  438.7 0.8 fusion.7
  439.5 1.0 pad_maximum_fusion
  440.6 0.0 reduce-scatter.2.cloned.1.call-update
  440.6 0.8 exponential_multiply_fusion
  441.3 55.5 %reduce-scatter.2.cloned.1.call-done = f32[256,64]{0,1:T(8,128)} async-done(((f32[256,1024]{0,1:T(8,128)}), f32[256,64]{0,1:T(8,128)}) %reduce-scatter.2.cloned.1.call-update) | async-done | bytes 65552 | tf_op jit(solution)/shard_map/reduce_scatter | solution.py:63
  496.9 1.5 multiply_convert_fusion.2
  (4 shorter events, 0.0 us)
Async XLA Ops:
  6.5 6.2 %copy-start = (f32[52,52]{1,0:T(8,128)S(1)}, f32[52,52]{1,0:T(8,128)}, u32[]{:S(2)}) copy-start(f32[52,52]{1,0:T(8,128)} %param.5) | copy-start | bytes 32452
  6.5 490.3 %reduce-scatter.2.cloned.1.call-start = ((), (), s32[]{:S(2)}) async-start(), calls=%async_computation.1 | async-start | bytes 1114112 | tf_op jit(solution)/shard_map/reduce_scatter | solution.py:63
  25.2 8.8 %copy-start.3 = (f32[256,1,3328]{0,2,1:T(8,128)}, f32[256,1,3328]{0,2,1:T(8,128)S(1)}, u32[]{:S(2)}) copy-start(f32[256,1,3328]{0,2,1:T(8,128)S(1)} %reshape.17) | copy-start | bytes 10223620
  25.2 14.6 %collective-permute-start = (f32[256,1,3328]{0,2,1:T(8,128)S(1)}, f32[256,1,3328]{0,2,1:T(8,128)}, u32[]{:S(2)}, u32[]{:S(2)}) collective-permute-start(f32[256,1,3328]{0,2,1:T(8,128)S(1)} %reshape.17), channel_id=1, source_target_pairs={{0,1},{1,0},{2,3},{3,2},{4,5},{5,4},{6,7},{7,6},{8,9},{9,8},{10,11... | collective-permute-start | bytes 10223624 | tf_op jit(solution)/shard_map/ppermute | solution.py:18
  43.2 1.9 copy-start.2
  43.3 76.9 %collective-permute-start.1 = (f32[256,1,3328]{0,2,1:T(8,128)S(1)}, f32[256,1,3328]{0,2,1:T(8,128)}, u32[]{:S(2)}, u32[]{:S(2)}) collective-permute-start(f32[256,1,3328]{0,2,1:T(8,128)S(1)} %add_select_fusion.2), channel_id=1, source_target_pairs={{0,2},{2,0},{1,3},{3,1},{4,6},{6,4},{5,7},{7,5},{8,10},{10,8},{9,1... | collective-permute-start | bytes 10223624 | tf_op jit(solution)/shard_map/ppermute | solution.py:18
  123.6 151.5 %collective-permute-start.2 = (f32[256,1,3328]{0,2,1:T(8,128)S(1)}, f32[256,1,3328]{0,2,1:T(8,128)}, u32[]{:S(2)}, u32[]{:S(2)}) collective-permute-start(f32[256,1,3328]{0,2,1:T(8,128)S(1)} %add_select_fusion.1), channel_id=1, source_target_pairs={{0,4},{4,0},{1,5},{5,1},{2,6},{6,2},{3,7},{7,3},{8,12},{12,8},{9,1... | collective-permute-start | bytes 10223624 | tf_op jit(solution)/shard_map/ppermute | solution.py:18
  279.5 153.9 %collective-permute-start.3 = (f32[256,1,3328]{0,2,1:T(8,128)}, f32[256,1,3328]{0,2,1:T(8,128)S(1)}, u32[]{:S(2)}, u32[]{:S(2)}) collective-permute-start(f32[256,1,3328]{0,2,1:T(8,128)} %add_select_fusion), channel_id=1, source_target_pairs={{0,8},{8,0},{1,9},{9,1},{2,10},{10,2},{3,11},{11,3},{4,12},{12,4},... | collective-permute-start | bytes 10223624 | tf_op jit(solution)/shard_map/ppermute | solution.py:18
  284.0 152.1 %copy-start.1 = (s32[3328,256]{1,0:T(8,128)S(1)}, s32[3328,256]{1,0:T(8,128)}, u32[]{:S(2)}) copy-start(s32[3328,256]{1,0:T(8,128)} %param.6) | copy-start | bytes 10223620
Sparse Core Ops, SparseCore 0:
  440.7 56.1 reduce-scatter.1
where the time goes:
time: 508 us; the launch traced here: 505 us
  waiting for transfers between devices  435 us (86%)
  other arithmetic  17.3 us (3%)
  starting transfers between devices  17.1 us (3%)
  between operations  13.6 us (3%)
  local copies, waits for them, and re-layouts  12.8 us (3%)
  matrix products  9.22 us (2%)
    ppermute x4, waiting for transfers between devices, partner_2(): return lax.ppermute(block, axis, route)  380 us
    reduce_scatter x1, waiting for transfers between devices, per_device(): lax.psum_scatter(partial_sums, 'tensor', scatter_dimension=1, tiled=True)  55.5 us
    ppermute x4, starting transfers between devices, partner_2(): return lax.ppermute(block, axis, route)  17.1 us
    select_n x3, other arithmetic, per_device(): values = jnp.where(upper, partner - values, values + partner)  11.2 us
  transfers between devices with their start and end apart: 5, of which 5 were waited for; matrix products, arithmetic and copies ran while one was open for 0% of the time, Pallas kernels for 0%

commit v1 on v0

v1 whole, which is shorter than its diff:
```python
import jax
import jax.numpy as jnp
from jax import lax
from jax.experimental import pallas as pl
from jax.experimental.pallas import tpu as pltpu
from jax.sharding import PartitionSpec as P

MESH = pl.DeviceIdType.MESH
NY, NX, NT = 8, 4, 16
ROWS = 256
HALF = ROWS // 2
INNER_M = 52
QUARTER = 832
QPAD = 896
SLICE = 208
TILE = 16
TILES = SLICE // TILE
PIECES = ((0, 112), (112, 96))
F32, BF16 = jnp.float32, jnp.bfloat16


def iota(shape, dim):
    return lax.broadcasted_iota(jnp.int32, shape, dim)


def kernel(
    acts, mix, codes, expo, out,
    xbuf, cbuf, mpad, gbuf, zbuf, s1, r1, s2, wbuf, ins, inr, pk, ces, cer, xs, xr, zs, zr, fs, fr,
    lsem, s1s, s1r, s2s, s2r, us, ur, ds, dr, iss, irs, css, crs, xss, xrs, zss, zrs, fss, frs,
):
    dp = lax.axis_index("dp")
    t = lax.axis_index("tensor")
    y, x = dp // NX, dp % NX
    z, core = t // 2, t % 2
    sib = t + 1 - 2 * core
    fy, jy = y % 2, y // 2
    up = ((y + 1) % NY) * NX + x
    down = ((y + NY - 1) % NY) * NX + x

    def along_t(dest):
        return (dp, dest)

    def along_x(dest):
        return (y * NX + dest, t)

    def rcopy(src, dst, ssem, rsem, dev):
        return pltpu.make_async_remote_copy(
            src_ref=src, dst_ref=dst, send_sem=ssem, recv_sem=rsem, device_id=dev, device_id_type=MESH
        )

    barrier = pltpu.get_barrier_semaphore()

    def greet(dev):
        pl.semaphore_signal(barrier, inc=1, device_id=dev, device_id_type=MESH)

    @pl.loop(1, NT)
    def _(o):
        greet(along_t((t + o) % NT))

    @pl.loop(1, NX)
    def _(o):
        greet(along_x((x + o) % NX))

    greet((up, t))
    greet((down, t))

    row0 = pl.multiple_of(x * QUARTER + jy * SLICE, 16)
    get_codes = pltpu.make_async_copy(codes.at[pl.ds(row0, SLICE)], cbuf, lsem.at[0])
    get_codes.start()
    get_acts = pltpu.make_async_copy(acts, xbuf, lsem.at[1])
    get_acts.start()
    get_codes.wait()
    for h in range(2):
        shift = 28 - 4 * (h + 2 * fy)
        field = jnp.right_shift(jnp.left_shift(cbuf[...], shift), 28)
        s1[h] = field.astype(F32).astype(BF16).reshape(TILES, TILE, 256)
    pl.semaphore_wait(barrier, NT - 1 + NX - 1 + 2)

    def first(h, i):
        return rcopy(s1.at[h, i], r1.at[h, t], s1s.at[h, i], s1r.at[h, t], along_t(i + 3 * h))

    for h in range(2):

        @pl.loop(0, TILES)
        def _(o):
            i = (t + o) % TILES

            @pl.when(i + 3 * h != t)
            def _():
                first(h, i).start()

    mpad[...] = jnp.zeros_like(mpad)
    mpad[0:INNER_M, 0:INNER_M] = mix[...]

    def block_of(v):
        return jnp.right_shift(v * 1261, 16)

    both = jnp.bitwise_and(iota((128, 128), 0), iota((128, 128), 1))
    both = jnp.bitwise_xor(both, jnp.right_shift(both, 2))
    both = jnp.bitwise_xor(both, jnp.right_shift(both, 1))
    had = (1 - 2 * jnp.bitwise_and(both, 1)).astype(F32).astype(BF16)
    cols = iota((128, QPAD), 1)
    inside = cols < QUARTER
    cblock = block_of(cols)
    which = iota((128, QPAD), 0)
    col_block = jnp.where(inside & (cblock == which), 1.0, 0.0).astype(BF16)
    col_inner = jnp.where(inside & (cols - INNER_M * cblock == which), 1.0, 0.0).astype(BF16)
    mixing = mpad[...].astype(BF16)
    right_m = jnp.dot(mixing, col_inner, preferred_element_type=F32).astype(BF16)
    right_h = jnp.dot(had, col_block, preferred_element_type=F32).astype(BF16)

    @pl.loop(0, 4)
    def _(blk):
        at = pl.multiple_of(blk * 240, 16)
        rows = iota((240, 128), 0) + (at - 64)
        ok = (rows >= 0) & (rows < QUARTER)
        rblock = block_of(rows)
        lane = iota((240, 128), 1)
        row_block = jnp.where(ok & (rblock == lane), 1.0, 0.0).astype(BF16)
        row_inner = jnp.where(ok & (rows - INNER_M * rblock == lane), 1.0, 0.0).astype(BF16)
        m_part = jnp.dot(row_inner, right_m, preferred_element_type=F32)
        h_part = jnp.dot(row_block, right_h, preferred_element_type=F32)
        gbuf[pl.ds(at, 240)] = (m_part * h_part).astype(BF16)

    get_acts.wait()
    for q in range(4):
        lo = q * QUARTER - 64 * (q % 2)
        g = gbuf[0:QPAD] if q % 2 else gbuf[64 : 64 + QPAD]
        zbuf[q] = jnp.dot(xbuf[:, lo : lo + QPAD], g, preferred_element_type=F32)

    @pl.loop(0, ROWS // 16)
    def _(blk):
        rows = pl.ds(pl.multiple_of(blk * 16, 16), 16)
        z0, z1, z2, z3 = (zbuf[q, rows, :] for q in range(4))
        u0, u1, u2, u3 = z0 + z1, z0 - z1, z2 + z3, z2 - z3
        for q, v in enumerate((u0 + u2, u1 + u3, u0 - u2, u1 - u3)):
            ins[q, rows, :] = (v * 0.125).astype(BF16)

    def spread(q):
        return rcopy(ins.at[q], inr.at[x], iss.at[q], irs.at[x], along_x(q))

    for d in (2, 1, 3):
        spread((x + d) % NX).start()
    inr[x] = ins[x]

    def tile_at(h, i):
        return wbuf.at[h, fy, pl.ds(pl.multiple_of(jy * SLICE + i * TILE, 16), TILE)]

    def second(h, a):
        i = t - 3 * h
        return rcopy(s2.at[h, a], tile_at(h, i), s2s.at[h, a], s2r.at[h, i], along_t(a))

    def mine(h):
        i = t - 3 * h
        return (i >= 0) & (i < TILES)

    for f in range(2):
        for h in range(2):
            wbuf[h, f, QUARTER:QPAD, :] = jnp.zeros((QPAD - QUARTER, 256), BF16)

    for h in range(2):

        @pl.when(mine(h))
        def _():
            @pl.loop(1, NT)
            def _(o):
                b = (t + o) % NT
                rcopy(s1.at[h, 0], r1.at[h, b], s1s.at[h, 0], s1r.at[h, b], along_t(b)).wait_recv()

            r1[h, t] = s1[h, t - 3 * h]
            for half in range(2):
                lanes = slice(128 * half, 128 * half + 128)
                v = [r1[h, b, :, lanes].astype(F32) for b in range(NT)]
                for bit in (1, 2, 4, 8):
                    v = [v[a ^ bit] - v[a] if a & bit else v[a] + v[a ^ bit] for a in range(NT)]
                for a in range(NT):
                    s2[h, a, :, lanes] = v[a].astype(BF16)

            @pl.loop(1, NT)
            def _(o):
                second(h, (t + o) % NT).start()

            wbuf[h, fy, pl.ds(pl.multiple_of(jy * SLICE + (t - 3 * h) * TILE, 16), TILE), :] = s2[h, t]

    def assembled(h):
        @pl.loop(0, TILES)
        def _(i):
            @pl.when(i + 3 * h != t)
            def _():
                rcopy(s2.at[h, 0], tile_at(h, i), s2s.at[h, 0], s2r.at[h, i], along_t(i + 3 * h)).wait_recv()

    def ring(h, step, piece, sign):
        yy = (y - sign * step + NY) % NY
        off, size = PIECES[piece]
        part = wbuf.at[h, yy % 2, pl.ds(pl.multiple_of((yy // 2) * SLICE + off, 16), size)]
        if sign > 0:
            return rcopy(part, part, us.at[h, step, piece], ur.at[h, step, piece], (up, t))
        return rcopy(part, part, ds.at[h, step, piece], dr.at[h, step, piece], (down, t))

    def arrived(h, step, piece, sign):
        yy = (y - sign * (step + 1) + NY) % NY
        off, size = PIECES[piece]
        part = wbuf.at[h, yy % 2, pl.ds(pl.multiple_of((yy // 2) * SLICE + off, 16), size)]
        if sign > 0:
            rcopy(part, part, us.at[h, step, piece], ur.at[h, step, piece], (up, t)).wait_recv()
        else:
            rcopy(part, part, ds.at[h, step, piece], dr.at[h, step, piece], (down, t)).wait_recv()

    def ring_start(h):
        for piece in range(2):
            ring(h, 0, piece, 1).start()
            ring(h, 0, piece, -1).start()

    def ring_step(h, s):
        if s == 4:
            arrived(h, 3, 0, 1)
            arrived(h, 3, 1, -1)
            return
        for piece in range(2):
            arrived(h, s - 1, piece, 1)
            if s < 3 or piece == 0:
                ring(h, s, piece, 1).start()
            arrived(h, s - 1, piece, -1)
            if s < 3 or piece == 1:
                ring(h, s, piece, -1).start()

    def product(h, half_of):
        rows = pl.ds(pl.multiple_of(half_of * HALF, HALF), HALF)
        lhs = inr[:, rows, :].reshape(NX * HALF, QPAD)
        return [
            jnp.dot(lhs, wbuf[h, f], preferred_element_type=F32).reshape(NX, HALF, 256) for f in range(2)
        ]

    def swap_cores(h):
        return rcopy(ces.at[h], cer.at[h], css.at[h], crs.at[h], along_t(sib))

    def partials(h):
        for f, v in enumerate(product(h, 1 - core)):
            ces[h, :, :, 256 * f : 256 * f + 256] = v.astype(BF16)
        swap_cores(h).start()
        for f, v in enumerate(product(h, core)):
            pk[h, :, :, 256 * f : 256 * f + 256] = v

    def over_x(h, p):
        return rcopy(xs.at[h, p], xr.at[h, x], xss.at[h, p], xrs.at[h, x], along_x(p))

    def reduce_x(h):
        swap_cores(h).wait_recv()

        @pl.loop(0, NX)
        def _(p):
            v = pk[h, p] + cer[h, p].astype(F32)
            pk[h, p] = v
            xs[h, p] = v.astype(BF16)

        for d in (2, 1, 3):
            over_x(h, (x + d) % NX).start()

    def chip_of(h, i):
        return 2 * h + 4 * (i // 2) + i % 2

    def over_z(h, i):
        dest = 2 * chip_of(h, i) + core
        return rcopy(zs.at[h, i], zr.at[z], zss.at[h, i], zrs.at[z], along_t(dest))

    def reduce_z(h):
        for d in (1, 3, 2):
            src = (x + d) % NX
            rcopy(xs.at[h, 0], xr.at[h, src], xss.at[h, 0], xrs.at[h, src], along_x(src)).wait_recv()
        total = pk[h, x]
        for d in (1, 2, 3):
            total = total + xr[h, (x + d) % NX].astype(F32)
        for i in range(4):
            zs[h, i] = total[:, 128 * i : 128 * i + 128].astype(BF16)
        for i in range(4):

            @pl.when(chip_of(h, i) != z)
            def _():
                over_z(h, i).start()

            @pl.when(chip_of(h, i) == z)
            def _():
                fs[...] = total[:, 128 * i : 128 * i + 128]

    assembled(0)
    ring_start(0)
    ring_step(0, 1)
    ring_step(0, 2)
    assembled(1)
    ring_step(0, 3)
    ring_start(1)
    ring_step(0, 4)
    ring_step(1, 1)
    ring_step(1, 2)
    for d in (1, 3, 2):
        src = (x + d) % NX
        rcopy(ins.at[0], inr.at[src], iss.at[0], irs.at[src], along_x(src)).wait_recv()
    partials(0)
    ring_step(1, 3)
    reduce_x(0)
    ring_step(1, 4)
    partials(1)
    reduce_z(0)
    reduce_x(1)
    reduce_z(1)

    def total_of_z(o, acc):
        src = (z + o) % 8
        rcopy(zs.at[0, 0], zr.at[src], zss.at[0, 0], zrs.at[src], along_t(2 * src + core)).wait_recv()
        return acc + zr[src].astype(F32)

    total = lax.fori_loop(1, 8, total_of_z, fs[...])
    two = jnp.left_shift(jnp.ones((1, 128), jnp.int32), expo[pl.ds(z, 1), :] + 16)
    total = total * (two.astype(F32) * (2.0 ** -28))
    fs[...] = total
    last = rcopy(fs, fr, fss, frs, along_t(sib))
    last.start()

    def own_columns(v):
        return jnp.where(core == 1, v[:, 64:], v[:, :64]).astype(BF16)

    out[pl.ds(pl.multiple_of(core * HALF, HALF), HALF), :] = own_columns(total)
    last.wait_recv()
    out[pl.ds(pl.multiple_of((1 - core) * HALF, HALF), HALF), :] = own_columns(fr[...])

    last.wait_send()
    for h in range(2):

        @pl.loop(0, TILES)
        def _(i):
            @pl.when(i + 3 * h != t)
            def _():
                first(h, i).wait_send()

        @pl.when(mine(h))
        def _():
            @pl.loop(1, NT)
            def _(o):
                second(h, (t + o) % NT).wait_send()

        for s in range(4):
            for piece in range(2):
                if s < 3 or piece == 0:
                    ring(h, s, piece, 1).wait_send()
                if s < 3 or piece == 1:
                    ring(h, s, piece, -1).wait_send()
        swap_cores(h).wait_send()
        for d in (1, 2, 3):
            over_x(h, (x + d) % NX).wait_send()
        for i in range(4):

            @pl.when(chip_of(h, i) != z)
            def _():
                over_z(h, i).wait_send()

    for d in (1, 2, 3):
        spread((x + d) % NX).wait_send()


def per_device(hidden_acts, mixing, packed_codes, exponents):
    vmem = pltpu.VMEM
    dma = pltpu.SemaphoreType.DMA
    scratch = [
        vmem((ROWS, 3328), BF16),
        vmem((SLICE, 256), jnp.int32),
        vmem((128, 128), F32),
        vmem((QPAD + 64, QPAD), BF16),
        vmem((4, ROWS, QPAD), F32),
        vmem((2, TILES, TILE, 256), BF16),
        vmem((2, NT, TILE, 256), BF16),
        vmem((2, NT, TILE, 256), BF16),
        vmem((2, 2, QPAD, 256), BF16),
        vmem((NX, ROWS, QPAD), BF16),
        vmem((NX, ROWS, QPAD), BF16),
        vmem((2, NX, HALF, 512), F32),
        vmem((2, NX, HALF, 512), BF16),
        vmem((2, NX, HALF, 512), BF16),
        vmem((2, NX, HALF, 512), BF16),
        vmem((2, NX, HALF, 512), BF16),
        vmem((2, 4, HALF, 128), BF16),
        vmem((8, HALF, 128), BF16),
        vmem((HALF, 128), F32),
        vmem((HALF, 128), F32),
        dma((2,)),
        dma((2, TILES)), dma((2, NT)),
        dma((2, NT)), dma((2, TILES)),
        dma((2, 4, 2)), dma((2, 4, 2)), dma((2, 4, 2)), dma((2, 4, 2)),
        dma((NX,)), dma((NX,)),
        dma((2,)), dma((2,)),
        dma((2, NX)), dma((2, NX)),
        dma((2, 4)), dma((8,)),
        dma(()), dma(()),
    ]
    any_, in_vmem = pl.BlockSpec(memory_space=pl.ANY), pl.BlockSpec(memory_space=pltpu.VMEM)
    return pl.pallas_call(
        kernel,
        out_shape=jax.ShapeDtypeStruct((ROWS, 64), BF16),
        in_specs=[any_, in_vmem, any_, in_vmem],
        out_specs=in_vmem,
        scratch_shapes=scratch,
        compiler_params=pltpu.CompilerParams(
            collective_id=0, has_side_effects=True, vmem_limit_bytes=48 * 2**20
        ),
        name="rotated_projection",
    )(hidden_acts, mixing, packed_codes, exponents.reshape(8, 128))


def solution(mesh):
    placed = (P("dp", "tensor"), P(), P("tensor", None), P())
    return jax.shard_map(
        per_device, mesh=mesh, in_specs=placed, out_specs=P("dp", "tensor"), check_vma=False
    )
```

time: 508 us -> 79.4 us (0.16)
  the two profiles are of different devices: /device:TPU:1 before, /device:TPU:131 now
where the time goes in v1:
time: 79.4 us; the launch traced here: 79.1 us
  Pallas kernels  73.5 us (93%)
  local copies, waits for them, and re-layouts  5.56 us (7%)
    pallas_call x1, Pallas kernels, per_device(): pl.pallas_call(kernel, out_shape=jax.ShapeDtypeStruct((ROWS, 64), BF16),...  73.5 us
    unnamed x8, local copies, waits for them, and re-layouts  4.85 us

profile of v1, /device:TPU:131, one launch (start us, length us, event | category | flops | bytes accessed | tf_op | source)
XLA Modules:
  0.0 79.1 jit_solution(13560650789412384961)
XLA Ops:
  0.0 0.0 copy-start
  0.0 2.0 %copy-done = s32[3328,256]{1,0:T(8,128)S(1)} copy-done((s32[3328,256]{1,0:T(8,128)S(1)}, s32[3328,256]{1,0:T(8,128)}, u32[]{:S(2)}) %copy-start) | copy-done | bytes 3407896
  2.0 0.0 copy-start.1
  2.0 1.5 %copy-done.1 = bf16[256,3328]{1,0:T(8,128)(2,1)S(1)} copy-done((bf16[256,3328]{1,0:T(8,128)(2,1)S(1)}, bf16[256,3328]{1,0:T(8,128)(2,1)}, u32[]{:S(2)}) %copy-start.1) | copy-done | bytes 1703960
  3.4 0.0 copy-start.2
  3.4 0.7 copy-done.2
  4.2 0.0 copy-start.3
  4.2 0.7 copy-done.3
  4.9 73.5 %rotated_projection.1 = bf16[256,64]{1,0:T(8,128)(2,1)S(1)} custom-call(bf16[256,3328]{1,0:T(8,128)(2,1)S(1)} %copy-done.1, f32[52,52]{1,0:T(8,128)S(1)} %copy-done.2, s32[3328,256]{1,0:T(8,128)S(1)} %copy-done, s32[8,128]{1,0:T(8,128)S(1)} %bitcast.1), custom_call_target="tpu_custom_call" | custom-call | tf_op jit(solution)/shard_map/rotated_projection/pallas_call | solution.py:395
  78.4 0.7 copy.5
Async XLA Ops:
  0.0 2.0 %copy-start = (s32[3328,256]{1,0:T(8,128)S(1)}, s32[3328,256]{1,0:T(8,128)}, u32[]{:S(2)}) copy-start(s32[3328,256]{1,0:T(8,128)} %codes.1) | copy-start | bytes 10223620
  2.0 1.5 %copy-start.1 = (bf16[256,3328]{1,0:T(8,128)(2,1)S(1)}, bf16[256,3328]{1,0:T(8,128)(2,1)}, u32[]{:S(2)}) copy-start(bf16[256,3328]{1,0:T(8,128)(2,1)} %acts.1) | copy-start | bytes 5111812
  3.4 0.7 copy-start.2
  4.2 0.7 copy-start.3

commit v2 on v0

v2 whole, which is shorter than its diff:
```python
import jax
import jax.numpy as jnp
from jax import lax
from jax.experimental import pallas as pl
from jax.experimental.pallas import tpu as pltpu
from jax.sharding import PartitionSpec as P

MESH = pl.DeviceIdType.MESH
NY, NX, NT = 8, 4, 16
ROWS = 256
HALF = ROWS // 2
INNER_M = 52
BLOCK = 3328
QUARTER = 832
QPAD = 896
SLICE = QPAD // NY
TILE = 16
TILES = SLICE // TILE
FIELDS = 4
COLS = 256
NEAR, FAR_UP, FAR_DOWN = (0, 112), (0, 64), (64, 48)
PARTS = ((0, 512), (512, 384))
F32, BF16 = jnp.float32, jnp.bfloat16


def iota(shape, dim):
    return lax.broadcasted_iota(jnp.int32, shape, dim)


def kernel(
    acts, mix, codes, expo, out,
    xbuf, cbuf, mixv, ebuf, mpad, gbuf, zbuf, s1, r1, s2, wbuf, ins, inr, pk, ces, cer, xs, xr, zs, zr, fs,
    lsem, s1s, s1r, s2s, s2r, us, ur, ds, dr, iss, irs, css, crs, xss, xrs, zss, zrs,
):
    dp = lax.axis_index("dp")
    t = lax.axis_index("tensor")
    y, x = dp // NX, dp % NX
    z, core = t // 2, t % 2
    sib = t + 1 - 2 * core
    up = ((y + 1) % NY) * NX + x
    down = ((y + NY - 1) % NY) * NX + x

    def along_t(dest):
        return (dp, dest)

    def along_x(dest):
        return (y * NX + dest, t)

    def rcopy(src, dst, ssem, rsem, dev):
        return pltpu.make_async_remote_copy(
            src_ref=src, dst_ref=dst, send_sem=ssem, recv_sem=rsem, device_id=dev, device_id_type=MESH
        )

    row0 = x * QUARTER + y * SLICE
    row1 = jnp.minimum(row0, BLOCK - SLICE)
    get_codes = pltpu.make_async_copy(
        codes.at[pl.ds(pl.multiple_of(row1, 16), SLICE)], cbuf.at[pl.ds(0, SLICE)], lsem.at[0]
    )
    get_acts = pltpu.make_async_copy(acts, xbuf, lsem.at[1])
    get_mix = pltpu.make_async_copy(mix, mixv, lsem.at[2])
    get_expo = pltpu.make_async_copy(expo, ebuf, lsem.at[3])
    get_codes.start()

    barrier = pltpu.get_barrier_semaphore()

    def greet(dev):
        pl.semaphore_signal(barrier, inc=1, device_id=dev, device_id_type=MESH)

    for o in range(1, NT):
        greet(along_t((t + o) % NT))
    for o in range(1, NX):
        greet(along_x((x + o) % NX))
    greet((up, t))
    greet((down, t))

    get_mix.start()
    get_acts.start()
    get_expo.start()
    cbuf[SLICE:, :] = jnp.zeros((64, COLS), jnp.int32)
    lane = iota((SLICE, 128), 1)
    get_codes.wait()
    words = cbuf[pl.ds(pl.multiple_of(row0 - row1, 16), SLICE), :]
    for k in range(FIELDS):
        field = jnp.right_shift(jnp.left_shift(words, 28 - 4 * k), 28).astype(F32)
        left, right = field[:, :128], field[:, 128:]
        for c, v in enumerate((
            jnp.where(lane < 64, left, pltpu.roll(right, 64, 1)),
            jnp.where(lane < 64, pltpu.roll(left, 64, 1), right),
        )):
            s1[k // 2, :, k % 2, :, 128 * c : 128 * c + 128] = v.astype(BF16).reshape(TILES, TILE, 128)
    pl.semaphore_wait(barrier, NT - 1 + NX - 1 + 2)

    def first(g, i):
        return rcopy(s1.at[g, i], r1.at[t], s1s.at[g, i], s1r.at[t], along_t(8 * g + i))

    for g in range(2):

        @pl.loop(0, TILES)
        def _(o):
            i = (t + o) % TILES

            @pl.when(8 * g + i != t)
            def _():
                first(g, i).start()

    mpad[...] = jnp.zeros_like(mpad)
    get_mix.wait()
    mpad[0:INNER_M, 0:INNER_M] = mixv[...]

    def block_of(v):
        return jnp.right_shift(v * 1261, 16)

    both = jnp.bitwise_and(iota((128, 128), 0), iota((128, 128), 1))
    both = jnp.bitwise_xor(both, jnp.right_shift(both, 2))
    both = jnp.bitwise_xor(both, jnp.right_shift(both, 1))
    had = (1 - 2 * jnp.bitwise_and(both, 1)).astype(F32).astype(BF16)
    cols = iota((128, QPAD), 1)
    inside = cols < QUARTER
    cblock = block_of(cols)
    which = iota((128, QPAD), 0)
    col_block = jnp.where(inside & (cblock == which), 1.0, 0.0).astype(BF16)
    col_inner = jnp.where(inside & (cols - INNER_M * cblock == which), 1.0, 0.0).astype(BF16)
    mixing = mpad[...].astype(BF16)
    right_m = jnp.dot(mixing, col_inner, preferred_element_type=F32).astype(BF16)
    right_h = jnp.dot(had, col_block, preferred_element_type=F32).astype(BF16)

    @pl.loop(0, 4)
    def _(blk):
        at = pl.multiple_of(blk * 240, 16)
        rows = iota((240, 128), 0) + (at - 64)
        ok = (rows >= 0) & (rows < QUARTER)
        rblock = block_of(rows)
        lane = iota((240, 128), 1)
        row_block = jnp.where(ok & (rblock == lane), 1.0, 0.0).astype(BF16)
        row_inner = jnp.where(ok & (rows - INNER_M * rblock == lane), 1.0, 0.0).astype(BF16)
        m_part = jnp.dot(row_inner, right_m, preferred_element_type=F32)
        h_part = jnp.dot(row_block, right_h, preferred_element_type=F32)
        gbuf[pl.ds(at, 240)] = (m_part * h_part).astype(BF16)

    get_acts.wait()

    def spread(q, part):
        lo, n = PARTS[part]
        cut = pl.ds(lo, n)
        return rcopy(
            ins.at[q, :, cut], inr.at[x, :, cut], iss.at[q, part], irs.at[x, part], along_x(q)
        )

    for part, (lo, n) in enumerate(PARTS):
        for q in range(4):
            at = q * QUARTER - 64 * (q % 2)
            g = gbuf[0:QPAD, lo : lo + n] if q % 2 else gbuf[64 : 64 + QPAD, lo : lo + n]
            zbuf[q, :, 0:n] = jnp.dot(xbuf[:, at : at + QPAD], g, preferred_element_type=F32)

        @pl.loop(0, ROWS // 16)
        def _(blk):
            rows = pl.ds(pl.multiple_of(blk * 16, 16), 16)
            z0, z1, z2, z3 = (zbuf[q, rows, 0:n] for q in range(4))
            u0, u1, u2, u3 = z0 + z1, z0 - z1, z2 + z3, z2 - z3
            for q, v in enumerate((u0 + u2, u1 + u3, u0 - u2, u1 - u3)):
                ins[q, rows, lo : lo + n] = (v * 0.125).astype(BF16)

        for d in (2, 1, 3):
            spread((x + d) % NX, part).start()

    g0, i0 = t // 8, t % 8

    def tile_at(g, i):
        return wbuf.at[pl.ds(2 * g, 2), pl.ds(pl.multiple_of(y * SLICE + i * TILE, 16), TILE)]

    def second(a):
        return rcopy(s2.at[a], tile_at(g0, i0), s2s.at[a], s2r.at[g0, i0], along_t(a))

    @pl.when(i0 < TILES)
    def _():
        @pl.loop(1, NT)
        def _(o):
            b = (t + o) % NT
            rcopy(s1.at[0, 0], r1.at[b], s1s.at[0, 0], s1r.at[b], along_t(b)).wait_recv()

        r1[t] = s1[g0, i0]
        for f in range(2):
            for half in range(2):
                lanes = slice(128 * half, 128 * half + 128)
                v = [r1[b, f, :, lanes].astype(F32) for b in range(NT)]
                for bit in (1, 2, 4, 8):
                    v = [v[a ^ bit] - v[a] if a & bit else v[a] + v[a ^ bit] for a in range(NT)]
                for a in range(NT):
                    s2[a, f, :, lanes] = v[a].astype(BF16)

        @pl.loop(1, NT)
        def _(o):
            second((t + o) % NT).start()

        for f in range(2):
            wbuf[2 * g0 + f, pl.ds(pl.multiple_of(y * SLICE + i0 * TILE, 16), TILE), :] = s2[t, f]

    inr[x] = ins[x]

    def assembled(g):
        @pl.loop(0, TILES)
        def _(i):
            @pl.when(8 * g + i != t)
            def _():
                rcopy(s2.at[0], tile_at(g, i), s2s.at[0], s2r.at[g, i], along_t(8 * g + i)).wait_recv()

    def hop(k, step, sign, away):
        yy = (y - sign * away + NY) % NY
        off, n = NEAR if step < 3 else FAR_UP if sign > 0 else FAR_DOWN
        part = wbuf.at[k, pl.ds(pl.multiple_of(yy * SLICE + off, 16), n)]
        if sign > 0:
            return rcopy(part, part, us.at[k, step], ur.at[k, step], (up, t))
        return rcopy(part, part, ds.at[k, step], dr.at[k, step], (down, t))

    def ring(k, s):
        for sign in (1, -1):
            if s:
                hop(k, s - 1, sign, s).wait_recv()
            if s < 4:
                hop(k, s, sign, s).start()

    def swap_cores(k):
        return rcopy(ces.at[k], cer.at[k], css.at[k], crs.at[k], along_t(sib))

    def partials(k):
        w = wbuf[k]
        for p in range(NX):
            v = jnp.dot(inr[p], w, preferred_element_type=F32)
            ces[k, p] = jnp.where(core == 0, v[:, 128:], v[:, :128]).astype(BF16)
            pk[k, p] = jnp.where(core == 0, v[:, :128], v[:, 128:])
        swap_cores(k).start()

    def over_x(k, p):
        return rcopy(xs.at[k, p], xr.at[k, x], xss.at[k, p], xrs.at[k, x], along_x(p))

    def reduce_x(k):
        swap_cores(k).wait_recv()
        for p in range(NX):
            v = pk[k, p] + cer[k, p].astype(F32)
            pk[k, p] = v
            xs[k, p] = v.astype(BF16)
        for d in (2, 1, 3):
            over_x(k, (x + d) % NX).start()

    def over_z(k, i):
        return rcopy(zs.at[k, i], zr.at[z], zss.at[k, i], zrs.at[z], along_t(2 * (2 * k + i) + core))

    lane1 = iota((HALF, 128), 1)

    def reduce_z(k):
        for d in (1, 3, 2):
            src = (x + d) % NX
            rcopy(xs.at[k, 0], xr.at[k, src], xss.at[k, 0], xrs.at[k, src], along_x(src)).wait_recv()
        total = pk[k, x]
        for d in (1, 2, 3):
            total = total + xr[k, (x + d) % NX].astype(F32)
        top, low = total[:HALF], total[HALF:]
        packed = (
            jnp.where(lane1 < 64, top, pltpu.roll(low, 64, 1)),
            jnp.where(lane1 < 64, pltpu.roll(top, 64, 1), low),
        )
        for i in range(2):
            zs[k, i] = packed[i].astype(BF16)

            @pl.when(2 * k + i != z)
            def _():
                over_z(k, i).start()

            @pl.when(2 * k + i == z)
            def _():
                fs[...] = packed[i]

    assembled(0)
    ring(0, 0)
    ring(1, 0)
    assembled(1)
    ring(2, 0)
    ring(0, 1)
    ring(3, 0)
    ring(1, 1)
    ring(2, 1)
    ring(0, 2)
    ring(3, 1)
    ring(1, 2)
    ring(2, 2)
    ring(0, 3)
    ring(3, 2)
    ring(1, 3)
    ring(2, 3)
    for d in (1, 3, 2):
        src = (x + d) % NX
        for part, (lo, n) in enumerate(PARTS):
            cut = pl.ds(lo, n)
            rcopy(
                ins.at[0, :, cut], inr.at[src, :, cut], iss.at[0, part], irs.at[src, part], along_x(src)
            ).wait_recv()
    ring(0, 4)
    partials(0)
    ring(3, 3)
    ring(1, 4)
    reduce_x(0)
    partials(1)
    ring(2, 4)
    reduce_x(1)
    partials(2)
    ring(3, 4)
    reduce_x(2)
    partials(3)
    reduce_z(0)
    reduce_x(3)

    for g in range(2):

        @pl.loop(0, TILES)
        def _(i):
            @pl.when(8 * g + i != t)
            def _():
                first(g, i).wait_send()

    @pl.when(i0 < TILES)
    def _():
        @pl.loop(1, NT)
        def _(o):
            second((t + o) % NT).wait_send()

    for d in (1, 2, 3):
        for part in range(2):
            spread((x + d) % NX, part).wait_send()
    for k in range(FIELDS):
        for s in range(4):
            hop(k, s, 1, s).wait_send()
            hop(k, s, -1, s).wait_send()
        swap_cores(k).wait_send()

    reduce_z(1)
    reduce_z(2)
    reduce_z(3)
    for k in range(FIELDS):
        for d in (1, 2, 3):
            over_x(k, (x + d) % NX).wait_send()

    get_expo.wait()
    lane8 = iota((8, 128), 1)
    e = ebuf[...]
    mpad[0:8, :] = jnp.where(
        (lane8 < 64) == (core == 0), jnp.left_shift(1, e + 16), jnp.left_shift(1, pltpu.roll(e, 64, 1) + 16)
    ).astype(F32)

    def total_of_z(o, acc):
        src = (z + o) % 8
        rcopy(zs.at[0, 0], zr.at[src], zss.at[0, 0], zrs.at[src], along_t(2 * src + core)).wait_recv()
        return acc + zr[src].astype(F32)

    total = lax.fori_loop(1, 8, total_of_z, fs[...])
    total = total * (mpad[pl.ds(z, 1), :] * (2.0 ** -28))
    out[0:HALF, :] = total[:, :64].astype(BF16)
    out[HALF:ROWS, :] = pltpu.roll(total, 64, 1)[:, :64].astype(BF16)
    for k in range(FIELDS):
        for i in range(2):

            @pl.when(2 * k + i != z)
            def _():
                over_z(k, i).wait_send()


def per_device(hidden_acts, mixing, packed_codes, exponents):
    vmem = pltpu.VMEM
    dma = pltpu.SemaphoreType.DMA
    scratch = [
        vmem((ROWS, BLOCK), BF16),
        vmem((SLICE + 64, COLS), jnp.int32),
        vmem((INNER_M, INNER_M), F32),
        vmem((8, 128), jnp.int32),
        vmem((128, 128), F32),
        vmem((QPAD + 64, QPAD), BF16),
        vmem((4, ROWS, 512), F32),
        vmem((2, TILES, 2, TILE, COLS), BF16),
        vmem((NT, 2, TILE, COLS), BF16),
        vmem((NT, 2, TILE, COLS), BF16),
        vmem((FIELDS, QPAD, COLS), BF16),
        vmem((NX, ROWS, QPAD), BF16),
        vmem((NX, ROWS, QPAD), BF16),
        vmem((FIELDS, NX, ROWS, 128), F32),
        vmem((FIELDS, NX, ROWS, 128), BF16),
        vmem((FIELDS, NX, ROWS, 128), BF16),
        vmem((FIELDS, NX, ROWS, 128), BF16),
        vmem((FIELDS, NX, ROWS, 128), BF16),
        vmem((FIELDS, 2, HALF, 128), BF16),
        vmem((8, HALF, 128), BF16),
        vmem((HALF, 128), F32),
        dma((4,)),
        dma((2, TILES)), dma((NT,)),
        dma((NT,)), dma((2, TILES)),
        dma((FIELDS, 4)), dma((FIELDS, 4)), dma((FIELDS, 4)), dma((FIELDS, 4)),
        dma((NX, 2)), dma((NX, 2)),
        dma((FIELDS,)), dma((FIELDS,)),
        dma((FIELDS, NX)), dma((FIELDS, NX)),
        dma((FIELDS, 2)), dma((8,)),
    ]
    in_hbm, in_vmem = pl.BlockSpec(memory_space=pltpu.HBM), pl.BlockSpec(memory_space=pltpu.VMEM)
    return pl.pallas_call(
        kernel,
        out_shape=jax.ShapeDtypeStruct((ROWS, 64), BF16),
        in_specs=[in_hbm] * 4,
        out_specs=in_vmem,
        scratch_shapes=scratch,
        compiler_params=pltpu.CompilerParams(
            collective_id=0, has_side_effects=True, vmem_limit_bytes=62 * 2**20
        ),
        name="rotated_projection",
    )(hidden_acts, mixing, packed_codes, exponents.reshape(8, 128))


def solution(mesh):
    placed = (P("dp", "tensor"), P(), P("tensor", None), P())
    return jax.shard_map(
        per_device, mesh=mesh, in_specs=placed, out_specs=P("dp", "tensor"), check_vma=False
    )
```

time: 508 us -> 71.8 us (0.14)
  waiting for transfers between devices: 435 us -> 0 us
  Pallas kernels: 0 us -> 70.1 us
  other arithmetic: 17.3 us -> 0 us
  starting transfers between devices: 17.1 us -> 0 us
  between operations: 13.6 us -> 0.01 us
  local copies, waits for them, and re-layouts: 12.8 us -> 1.54 us
  matrix products: 9.22 us -> 0 us
    ppermute x4 -> x0, waiting for transfers between devices: 380 us -> none  [partner_2(): return lax.ppermute(block, axis, route)]
    pallas_call x0 -> x1, Pallas kernels: none -> 70.1 us  [per_device(): pl.pallas_call(kernel, out_shape=jax.ShapeDtypeStruct((ROWS, 64), BF16),...]
    reduce_scatter x1 -> x0, waiting for transfers between devices: 55.5 us -> none  [per_device(): lax.psum_scatter(partial_sums, 'tensor', scatter_dimension=1, tiled=True)]
    ppermute x4 -> x0, starting transfers between devices: 17.1 us -> none  [partner_2(): return lax.ppermute(block, axis, route)]
    select_n x3 -> x0, other arithmetic: 11.2 us -> none  [per_device(): values = jnp.where(upper, partner - values, values + partner)]
    dot_general x6 -> x0, matrix products: 9.22 us -> none  [the longest x1 4.1 us: per_device(): jnp.einsum('xcg,cd->xdg', mixed, sylvester(INNER_H), precision=lax.Precis...]
    transpose x2 -> x0, local copies, waits for them, and re-layouts: 6.64 us -> none  [per_device(): jnp.einsum('rlb,lm->rmb', inner.astype(jnp.float32), sylvester(local_bloc...]
  transfers between devices with their start and end apart: 5 -> 0, of which waited for: 5 -> 0; matrix products, arithmetic and copies ran while one was open for 0% -> 0% of each run, Pallas kernels for 0% -> 0%
where the time goes in v2:
time: 71.8 us; the launch traced here: 71.6 us
  Pallas kernels  70.1 us (98%)
  local copies, waits for them, and re-layouts  1.54 us (2%)
    pallas_call x1, Pallas kernels, per_device(): pl.pallas_call(kernel, out_shape=jax.ShapeDtypeStruct((ROWS, 64), BF16),...  70.1 us
    pallas_call x1, local copies, waits for them, and re-layouts, per_device(): pl.pallas_call(kernel, out_shape=jax.ShapeDtypeStruct((ROWS, 64), BF16),...  1.54 us

profile of v2, /device:TPU:1, one launch (start us, length us, event | category | flops | bytes accessed | tf_op | source)
XLA Modules:
  0.0 71.6 jit_solution(424376734490338378)
XLA Ops:
  0.0 70.1 %rotated_projection.1 = bf16[256,64]{1,0:T(8,128)(2,1)} custom-call(bf16[256,3328]{1,0:T(8,128)(2,1)} %acts.1, f32[52,52]{1,0:T(8,128)} %mix.1, s32[3328,256]{1,0:T(8,128)} %codes.1, s32[8,128]{1,0:T(8,128)} %bitcast.1), custom_call_target="tpu_custom_call" | custom-call | tf_op jit(solution)/shard_map/rotated_projection/pallas_call | solution.py:401
  70.1 1.5 %copy.5 = bf16[256,64]{0,1:T(8,128)(2,1)} copy(bf16[256,64]{1,0:T(8,128)(2,1)} %rotated_projection.1) | data formatting | bytes 65536 | tf_op jit(solution)/shard_map/rotated_projection/pallas_call | solution.py:401

commit v3 on v2

--- a/solution.py
+++ b/solution.py
@@ -16,7 +16,7 @@
 SLICE = QPAD // NY
 TILE = 16
 TILES = SLICE // TILE
-FIELDS = 4
+CHUNKS = 4
 COLS = 256
 NEAR, FAR_UP, FAR_DOWN = (0, 112), (0, 64), (64, 48)
 PARTS = ((0, 512), (512, 384))
@@ -80,28 +80,33 @@
     lane = iota((SLICE, 128), 1)
     get_codes.wait()
     words = cbuf[pl.ds(pl.multiple_of(row0 - row1, 16), SLICE), :]
-    for k in range(FIELDS):
-        field = jnp.right_shift(jnp.left_shift(words, 28 - 4 * k), 28).astype(F32)
-        left, right = field[:, :128], field[:, 128:]
-        for c, v in enumerate((
-            jnp.where(lane < 64, left, pltpu.roll(right, 64, 1)),
-            jnp.where(lane < 64, pltpu.roll(left, 64, 1), right),
-        )):
-            s1[k // 2, :, k % 2, :, 128 * c : 128 * c + 128] = v.astype(BF16).reshape(TILES, TILE, 128)
+    fields = [jnp.right_shift(jnp.left_shift(words, 28 - 4 * f), 28).astype(F32) for f in range(4)]
+    for k in range(CHUNKS):
+        half = slice(128 * (k % 2), 128 * (k % 2) + 128)
+        left, right = fields[k // 2][:, half], fields[k // 2 + 2][:, half]
+        s1[k, :, :, 0:128] = (
+            jnp.where(lane < 64, left, pltpu.roll(right, 64, 1)).astype(BF16).reshape(TILES, TILE, 128)
+        )
+        s1[k, :, :, 128:256] = (
+            jnp.where(lane < 64, pltpu.roll(left, 64, 1), right).astype(BF16).reshape(TILES, TILE, 128)
+        )
     pl.semaphore_wait(barrier, NT - 1 + NX - 1 + 2)
 
-    def first(g, i):
-        return rcopy(s1.at[g, i], r1.at[t], s1s.at[g, i], s1r.at[t], along_t(8 * g + i))
-
-    for g in range(2):
+    def owner(k, i):
+        return (TILES * k + i) % NT
+
+    def first(k, i):
+        return rcopy(s1.at[k, i], r1.at[k, t], s1s.at[k, i], s1r.at[k, t], along_t(owner(k, i)))
+
+    for k in range(CHUNKS):
 
         @pl.loop(0, TILES)
         def _(o):
             i = (t + o) % TILES
 
-            @pl.when(8 * g + i != t)
-            def _():
-                first(g, i).start()
+            @pl.when(owner(k, i) != t)
+            def _():
+                first(k, i).start()
 
     mpad[...] = jnp.zeros_like(mpad)
     get_mix.wait()
@@ -163,46 +168,49 @@
         for d in (2, 1, 3):
             spread((x + d) % NX, part).start()
 
-    g0, i0 = t // 8, t % 8
-
-    def tile_at(g, i):
-        return wbuf.at[pl.ds(2 * g, 2), pl.ds(pl.multiple_of(y * SLICE + i * TILE, 16), TILE)]
-
-    def second(a):
-        return rcopy(s2.at[a], tile_at(g0, i0), s2s.at[a], s2r.at[g0, i0], along_t(a))
-
-    @pl.when(i0 < TILES)
-    def _():
-        @pl.loop(1, NT)
-        def _(o):
-            b = (t + o) % NT
-            rcopy(s1.at[0, 0], r1.at[b], s1s.at[0, 0], s1r.at[b], along_t(b)).wait_recv()
-
-        r1[t] = s1[g0, i0]
-        for f in range(2):
+    def tile_at(k, i):
+        return wbuf.at[k, pl.ds(pl.multiple_of(y * SLICE + i * TILE, 16), TILE)]
+
+    def mine(k):
+        return (t + 4 * NT - TILES * k) % NT
+
+    def second(k, a):
+        i = mine(k)
+        return rcopy(s2.at[k, a], tile_at(k, i), s2s.at[k, a], s2r.at[k, i], along_t(a))
+
+    for k in range(CHUNKS):
+
+        @pl.when(mine(k) < TILES)
+        def _():
+            @pl.loop(1, NT)
+            def _(o):
+                b = (t + o) % NT
+                rcopy(s1.at[k, 0], r1.at[k, b], s1s.at[k, 0], s1r.at[k, b], along_t(b)).wait_recv()
+
+            i = mine(k)
+            r1[k, t] = s1[k, i]
             for half in range(2):
                 lanes = slice(128 * half, 128 * half + 128)
-                v = [r1[b, f, :, lanes].astype(F32) for b in range(NT)]
+                v = [r1[k, b, :, lanes].astype(F32) for b in range(NT)]
                 for bit in (1, 2, 4, 8):
                     v = [v[a ^ bit] - v[a] if a & bit else v[a] + v[a ^ bit] for a in range(NT)]
                 for a in range(NT):
-                    s2[a, f, :, lanes] = v[a].astype(BF16)
-
-        @pl.loop(1, NT)
-        def _(o):
-            second((t + o) % NT).start()
-
-        for f in range(2):
-            wbuf[2 * g0 + f, pl.ds(pl.multiple_of(y * SLICE + i0 * TILE, 16), TILE), :] = s2[t, f]
+                    s2[k, a, :, lanes] = v[a].astype(BF16)
+
+            @pl.loop(1, NT)
+            def _(o):
+                second(k, (t + o) % NT).start()
+
+            wbuf[k, pl.ds(pl.multiple_of(y * SLICE + i * TILE, 16), TILE), :] = s2[k, t]
 
     inr[x] = ins[x]
 
-    def assembled(g):
+    def assembled(k):
         @pl.loop(0, TILES)
         def _(i):
-            @pl.when(8 * g + i != t)
-            def _():
-                rcopy(s2.at[0], tile_at(g, i), s2s.at[0], s2r.at[g, i], along_t(8 * g + i)).wait_recv()
+            @pl.when(owner(k, i) != t)
+            def _():
+                rcopy(s2.at[k, 0], tile_at(k, i), s2s.at[k, 0], s2r.at[k, i], along_t(owner(k, i))).wait_recv()
 
     def hop(k, step, sign, away):
         yy = (y - sign * away + NY) % NY
@@ -243,7 +251,7 @@
             over_x(k, (x + d) % NX).start()
 
     def over_z(k, i):
-        return rcopy(zs.at[k, i], zr.at[z], zss.at[k, i], zrs.at[z], along_t(2 * (2 * k + i) + core))
+        return rcopy(zs.at[k, i], zr.at[z], zss.at[k, i], zrs.at[z], along_t(2 * (k + 4 * i) + core))
 
     lane1 = iota((HALF, 128), 1)
 
@@ -262,31 +270,31 @@
         for i in range(2):
             zs[k, i] = packed[i].astype(BF16)
 
-            @pl.when(2 * k + i != z)
+            @pl.when(k + 4 * i != z)
             def _():
                 over_z(k, i).start()
 
-            @pl.when(2 * k + i == z)
+            @pl.when(k + 4 * i == z)
             def _():
                 fs[...] = packed[i]
 
     assembled(0)
     ring(0, 0)
+    assembled(1)
     ring(1, 0)
-    assembled(1)
+    assembled(2)
     ring(2, 0)
     ring(0, 1)
+    ring(1, 1)
+    assembled(3)
     ring(3, 0)
-    ring(1, 1)
+    ring(0, 2)
     ring(2, 1)
-    ring(0, 2)
+    ring(1, 2)
+    ring(0, 3)
     ring(3, 1)
-    ring(1, 2)
     ring(2, 2)
-    ring(0, 3)
-    ring(3, 2)
     ring(1, 3)
-    ring(2, 3)
     for d in (1, 3, 2):
         src = (x + d) % NX
         for part, (lo, n) in enumerate(PARTS):
@@ -296,37 +304,39 @@
             ).wait_recv()
     ring(0, 4)
     partials(0)
+    ring(3, 2)
+    reduce_x(0)
+    ring(2, 3)
+    ring(1, 4)
+    partials(1)
     ring(3, 3)
-    ring(1, 4)
-    reduce_x(0)
-    partials(1)
+    reduce_x(1)
     ring(2, 4)
-    reduce_x(1)
     partials(2)
+    reduce_x(2)
     ring(3, 4)
-    reduce_x(2)
     partials(3)
     reduce_z(0)
     reduce_x(3)
 
-    for g in range(2):
+    for k in range(CHUNKS):
 
         @pl.loop(0, TILES)
         def _(i):
-            @pl.when(8 * g + i != t)
-            def _():
-                first(g, i).wait_send()
-
-    @pl.when(i0 < TILES)
-    def _():
-        @pl.loop(1, NT)
-        def _(o):
-            second((t + o) % NT).wait_send()
+            @pl.when(owner(k, i) != t)
+            def _():
+                first(k, i).wait_send()
+
+        @pl.when(mine(k) < TILES)
+        def _():
+            @pl.loop(1, NT)
+            def _(o):
+                second(k, (t + o) % NT).wait_send()
 
     for d in (1, 2, 3):
         for part in range(2):
             spread((x + d) % NX, part).wait_send()
-    for k in range(FIELDS):
+    for k in range(CHUNKS):
         for s in range(4):
             hop(k, s, 1, s).wait_send()
             hop(k, s, -1, s).wait_send()
@@ -335,7 +345,7 @@
     reduce_z(1)
     reduce_z(2)
     reduce_z(3)
-    for k in range(FIELDS):
+    for k in range(CHUNKS):
         for d in (1, 2, 3):
             over_x(k, (x + d) % NX).wait_send()
 
@@ -353,12 +363,13 @@
 
     total = lax.fori_loop(1, 8, total_of_z, fs[...])
     total = total * (mpad[pl.ds(z, 1), :] * (2.0 ** -28))
-    out[0:HALF, :] = total[:, :64].astype(BF16)
-    out[HALF:ROWS, :] = pltpu.roll(total, 64, 1)[:, :64].astype(BF16)
-    for k in range(FIELDS):
+    turned = total.T
+    out[:, 0:HALF] = turned[0:64].astype(BF16)
+    out[:, HALF:ROWS] = turned[64:128].astype(BF16)
+    for k in range(CHUNKS):
         for i in range(2):
 
-            @pl.when(2 * k + i != z)
+            @pl.when(k + 4 * i != z)
             def _():
                 over_z(k, i).wait_send()
 
@@ -374,33 +385,33 @@
         vmem((128, 128), F32),
         vmem((QPAD + 64, QPAD), BF16),
         vmem((4, ROWS, 512), F32),
-        vmem((2, TILES, 2, TILE, COLS), BF16),
-        vmem((NT, 2, TILE, COLS), BF16),
-        vmem((NT, 2, TILE, COLS), BF16),
-        vmem((FIELDS, QPAD, COLS), BF16),
+        vmem((CHUNKS, TILES, TILE, COLS), BF16),
+        vmem((CHUNKS, NT, TILE, COLS), BF16),
+        vmem((CHUNKS, NT, TILE, COLS), BF16),
+        vmem((CHUNKS, QPAD, COLS), BF16),
         vmem((NX, ROWS, QPAD), BF16),
         vmem((NX, ROWS, QPAD), BF16),
-        vmem((FIELDS, NX, ROWS, 128), F32),
-        vmem((FIELDS, NX, ROWS, 128), BF16),
-        vmem((FIELDS, NX, ROWS, 128), BF16),
-        vmem((FIELDS, NX, ROWS, 128), BF16),
-        vmem((FIELDS, NX, ROWS, 128), BF16),
-        vmem((FIELDS, 2, HALF, 128), BF16),
+        vmem((CHUNKS, NX, ROWS, 128), F32),
+        vmem((CHUNKS, NX, ROWS, 128), BF16),
+        vmem((CHUNKS, NX, ROWS, 128), BF16),
+        vmem((CHUNKS, NX, ROWS, 128), BF16),
+        vmem((CHUNKS, NX, ROWS, 128), BF16),
+        vmem((CHUNKS, 2, HALF, 128), BF16),
         vmem((8, HALF, 128), BF16),
         vmem((HALF, 128), F32),
         dma((4,)),
-        dma((2, TILES)), dma((NT,)),
-        dma((NT,)), dma((2, TILES)),
-        dma((FIELDS, 4)), dma((FIELDS, 4)), dma((FIELDS, 4)), dma((FIELDS, 4)),
+        dma((CHUNKS, TILES)), dma((CHUNKS, NT)),
+        dma((CHUNKS, NT)), dma((CHUNKS, TILES)),
+        dma((CHUNKS, 4)), dma((CHUNKS, 4)), dma((CHUNKS, 4)), dma((CHUNKS, 4)),
         dma((NX, 2)), dma((NX, 2)),
-        dma((FIELDS,)), dma((FIELDS,)),
-        dma((FIELDS, NX)), dma((FIELDS, NX)),
-        dma((FIELDS, 2)), dma((8,)),
+        dma((CHUNKS,)), dma((CHUNKS,)),
+        dma((CHUNKS, NX)), dma((CHUNKS, NX)),
+        dma((CHUNKS, 2)), dma((8,)),
     ]
     in_hbm, in_vmem = pl.BlockSpec(memory_space=pltpu.HBM), pl.BlockSpec(memory_space=pltpu.VMEM)
     return pl.pallas_call(
         kernel,
-        out_shape=jax.ShapeDtypeStruct((ROWS, 64), BF16),
+        out_shape=jax.ShapeDtypeStruct((64, ROWS), BF16),
         in_specs=[in_hbm] * 4,
         out_specs=in_vmem,
         scratch_shapes=scratch,
@@ -408,7 +419,7 @@
             collective_id=0, has_side_effects=True, vmem_limit_bytes=62 * 2**20
         ),
         name="rotated_projection",
-    )(hidden_acts, mixing, packed_codes, exponents.reshape(8, 128))
+    )(hidden_acts, mixing, packed_codes, exponents.reshape(8, 128)).T
 
 
 def solution(mesh):

time: 71.8 us -> 65.1 us (0.907)
  Pallas kernels: 70.1 us -> 63 us
    pallas_call x1, Pallas kernels: 70.1 us -> 63 us  [per_device(): pl.pallas_call(kernel, out_shape=jax.ShapeDtypeStruct((64, ROWS), BF16),...]
    pallas_call x1 -> x0, local copies, waits for them, and re-layouts: 1.54 us -> none  [per_device(): pl.pallas_call(kernel, out_shape=jax.ShapeDtypeStruct((ROWS, 64), BF16),...]
    unnamed x0 -> x1, local copies, waits for them, and re-layouts: none -> 1.38 us
where the time goes in v3:
time: 65.1 us; the launch traced here: 64.4 us
  Pallas kernels  63 us (97%)
  local copies, waits for them, and re-layouts  1.38 us (2%)
    pallas_call x1, Pallas kernels, per_device(): pl.pallas_call(kernel, out_shape=jax.ShapeDtypeStruct((64, ROWS), BF16),...  63 us
    unnamed x1, local copies, waits for them, and re-layouts  1.38 us

profile of v3, /device:TPU:1, one launch (start us, length us, event | category | flops | bytes accessed | tf_op | source)
XLA Modules:
  0.0 64.4 jit_solution(18341134991581102286)
XLA Ops:
  0.0 63.0 %rotated_projection.1 = bf16[64,256]{1,0:T(8,128)(2,1)} custom-call(bf16[256,3328]{1,0:T(8,128)(2,1)} %acts.1, f32[52,52]{1,0:T(8,128)} %mix.1, s32[3328,256]{1,0:T(8,128)} %codes.1, s32[8,128]{1,0:T(8,128)} %bitcast.3), custom_call_target="tpu_custom_call" | custom-call | tf_op jit(solution)/shard_map/rotated_projection/pallas_call | solution.py:412
  63.0 1.4 %copy.6 = bf16[256,64]{0,1:T(8,128)(2,1)} copy(bf16[256,64]{0,1:T(8,128)(2,1)} %bitcast.2) | data formatting | bytes 65536

commit v4 on v3

--- a/solution.py
+++ b/solution.py
@@ -13,13 +13,15 @@
 BLOCK = 3328
 QUARTER = 832
 QPAD = 896
-SLICE = QPAD // NY
+TAKEN = 640
+REST = QUARTER - TAKEN
+DIRECT = 4 * REST
+SLICE = TAKEN // NY
 TILE = 16
 TILES = SLICE // TILE
 CHUNKS = 4
 COLS = 256
-NEAR, FAR_UP, FAR_DOWN = (0, 112), (0, 64), (64, 48)
-PARTS = ((0, 512), (512, 384))
+FAR = 48, 32
 F32, BF16 = jnp.float32, jnp.bfloat16
 
 
@@ -29,8 +31,9 @@
 
 def kernel(
     acts, mix, codes, expo, out,
-    xbuf, cbuf, mixv, ebuf, mpad, gbuf, zbuf, s1, r1, s2, wbuf, ins, inr, pk, ces, cer, xs, xr, zs, zr, fs,
-    lsem, s1s, s1r, s2s, s2r, us, ur, ds, dr, iss, irs, css, crs, xss, xrs, zss, zrs,
+    xbuf, cbuf, dbuf, mixv, ebuf, mpad, gbuf, zbuf, s1, r1, s2, wbuf, ins, inr, pk, ces, cer, xs, xr, zs, zr, fs,
+    own, acs, a1, a2, a3, pa, aces, acer,
+    lsem, s1s, s1r, s2s, s2r, us, ur, ds, dr, iss, irs, css, crs, xss, xrs, zss, zrs, a1s, a1r, a3s, a3r, asem,
 ):
     dp = lax.axis_index("dp")
     t = lax.axis_index("tensor")
@@ -51,14 +54,21 @@
             src_ref=src, dst_ref=dst, send_sem=ssem, recv_sem=rsem, device_id=dev, device_id_type=MESH
         )
 
-    row0 = x * QUARTER + y * SLICE
-    row1 = jnp.minimum(row0, BLOCK - SLICE)
-    get_codes = pltpu.make_async_copy(
-        codes.at[pl.ds(pl.multiple_of(row1, 16), SLICE)], cbuf.at[pl.ds(0, SLICE)], lsem.at[0]
-    )
+    row0 = pl.multiple_of(x * QUARTER + y * SLICE, 16)
+    get_codes = pltpu.make_async_copy(codes.at[pl.ds(row0, SLICE)], cbuf, lsem.at[0])
     get_acts = pltpu.make_async_copy(acts, xbuf, lsem.at[1])
     get_mix = pltpu.make_async_copy(mix, mixv, lsem.at[2])
     get_expo = pltpu.make_async_copy(expo, ebuf, lsem.at[3])
+    get_own = []
+    for u in range(2):
+        for at, row, n in (
+            (0, 2 * u * QUARTER + TAKEN, 192),
+            (192, (2 * u + 1) * QUARTER + TAKEN + 128, 64),
+            (256, (2 * u + 1) * QUARTER + TAKEN, 128),
+        ):
+            get_own.append(pltpu.make_async_copy(
+                codes.at[pl.ds(row, n)], dbuf.at[pl.ds(384 * u + at, n)], lsem.at[4 + len(get_own)]
+            ))
     get_codes.start()
 
     barrier = pltpu.get_barrier_semaphore()
@@ -76,38 +86,24 @@
     get_mix.start()
     get_acts.start()
     get_expo.start()
-    cbuf[SLICE:, :] = jnp.zeros((64, COLS), jnp.int32)
-    lane = iota((SLICE, 128), 1)
+    for g in get_own:
+        g.start()
     get_codes.wait()
-    words = cbuf[pl.ds(pl.multiple_of(row0 - row1, 16), SLICE), :]
-    fields = [jnp.right_shift(jnp.left_shift(words, 28 - 4 * f), 28).astype(F32) for f in range(4)]
-    for k in range(CHUNKS):
-        half = slice(128 * (k % 2), 128 * (k % 2) + 128)
-        left, right = fields[k // 2][:, half], fields[k // 2 + 2][:, half]
-        s1[k, :, :, 0:128] = (
-            jnp.where(lane < 64, left, pltpu.roll(right, 64, 1)).astype(BF16).reshape(TILES, TILE, 128)
-        )
-        s1[k, :, :, 128:256] = (
-            jnp.where(lane < 64, pltpu.roll(left, 64, 1), right).astype(BF16).reshape(TILES, TILE, 128)
-        )
-    pl.semaphore_wait(barrier, NT - 1 + NX - 1 + 2)
-
-    def owner(k, i):
-        return (TILES * k + i) % NT
-
-    def first(k, i):
-        return rcopy(s1.at[k, i], r1.at[k, t], s1s.at[k, i], s1r.at[k, t], along_t(owner(k, i)))
-
-    for k in range(CHUNKS):
-
-        @pl.loop(0, TILES)
-        def _(o):
-            i = (t + o) % TILES
-
-            @pl.when(owner(k, i) != t)
-            def _():
-                first(k, i).start()
-
+
+    def unpacked(words):
+        lane = iota((words.shape[0], 128), 1)
+        fields = [jnp.right_shift(jnp.left_shift(words, 28 - 4 * f), 28).astype(F32) for f in range(4)]
+        for k in range(CHUNKS):
+            half = slice(128 * (k % 2), 128 * (k % 2) + 128)
+            left, right = fields[k // 2][:, half], fields[k // 2 + 2][:, half]
+            yield (
+                jnp.where(lane < 64, left, pltpu.roll(right, 64, 1)).astype(BF16),
+                jnp.where(lane < 64, pltpu.roll(left, 64, 1), right).astype(BF16),
+            )
+
+    for k, halves in enumerate(unpacked(cbuf[...])):
+        for c in range(2):
+            s1[k, :, :, 128 * c : 128 * c + 128] = halves[c].reshape(TILES, TILE, 128)
     mpad[...] = jnp.zeros_like(mpad)
     get_mix.wait()
     mpad[0:INNER_M, 0:INNER_M] = mixv[...]
@@ -142,16 +138,30 @@
         h_part = jnp.dot(row_block, right_h, preferred_element_type=F32)
         gbuf[pl.ds(at, 240)] = (m_part * h_part).astype(BF16)
 
+    pl.semaphore_wait(barrier, NT - 1 + NX - 1 + 2)
+
+    def owner(k, i):
+        return (TILES * k + i) % NT
+
+    def first(k, i):
+        return rcopy(s1.at[k, i], r1.at[k, t], s1s.at[k, i], s1r.at[k, t], along_t(owner(k, i)))
+
+    for k in range(CHUNKS):
+
+        @pl.loop(0, TILES)
+        def _(o):
+            i = (t + o) % TILES
+
+            @pl.when(owner(k, i) != t)
+            def _():
+                first(k, i).start()
+
     get_acts.wait()
 
-    def spread(q, part):
-        lo, n = PARTS[part]
-        cut = pl.ds(lo, n)
-        return rcopy(
-            ins.at[q, :, cut], inr.at[x, :, cut], iss.at[q, part], irs.at[x, part], along_x(q)
-        )
-
-    for part, (lo, n) in enumerate(PARTS):
+    def spread(q):
+        return rcopy(ins.at[q], inr.at[x], iss.at[q], irs.at[x], along_x(q))
+
+    def inner(lo, n, put):
         for q in range(4):
             at = q * QUARTER - 64 * (q % 2)
             g = gbuf[0:QPAD, lo : lo + n] if q % 2 else gbuf[64 : 64 + QPAD, lo : lo + n]
@@ -162,11 +172,15 @@
             rows = pl.ds(pl.multiple_of(blk * 16, 16), 16)
             z0, z1, z2, z3 = (zbuf[q, rows, 0:n] for q in range(4))
             u0, u1, u2, u3 = z0 + z1, z0 - z1, z2 + z3, z2 - z3
-            for q, v in enumerate((u0 + u2, u1 + u3, u0 - u2, u1 - u3)):
-                ins[q, rows, lo : lo + n] = (v * 0.125).astype(BF16)
-
-        for d in (2, 1, 3):
-            spread((x + d) % NX, part).start()
+            put(blk, rows, [v * 0.125 for v in (u0 + u2, u1 + u3, u0 - u2, u1 - u3)])
+
+    def put_taken(blk, rows, quarters):
+        for q, v in enumerate(quarters):
+            ins[q, rows, :] = v.astype(BF16)
+
+    inner(0, TAKEN, put_taken)
+    for d in (2, 1, 3):
+        spread((x + d) % NX).start()
 
     def tile_at(k, i):
         return wbuf.at[k, pl.ds(pl.multiple_of(y * SLICE + i * TILE, 16), TILE)]
@@ -177,6 +191,11 @@
     def second(k, a):
         i = mine(k)
         return rcopy(s2.at[k, a], tile_at(k, i), s2s.at[k, a], s2r.at[k, i], along_t(a))
+
+    def butterfly(v):
+        for bit in (1, 2, 4, 8):
+            v = [v[a ^ bit] - v[a] if a & bit else v[a] + v[a ^ bit] for a in range(NT)]
+        return v
 
     for k in range(CHUNKS):
 
@@ -191,11 +210,8 @@
             r1[k, t] = s1[k, i]
             for half in range(2):
                 lanes = slice(128 * half, 128 * half + 128)
-                v = [r1[k, b, :, lanes].astype(F32) for b in range(NT)]
-                for bit in (1, 2, 4, 8):
-                    v = [v[a ^ bit] - v[a] if a & bit else v[a] + v[a ^ bit] for a in range(NT)]
-                for a in range(NT):
-                    s2[k, a, :, lanes] = v[a].astype(BF16)
+                for a, v in enumerate(butterfly([r1[k, b, :, lanes].astype(F32) for b in range(NT)])):
+                    s2[k, a, :, lanes] = v.astype(BF16)
 
             @pl.loop(1, NT)
             def _(o):
@@ -203,7 +219,80 @@
 
             wbuf[k, pl.ds(pl.multiple_of(y * SLICE + i * TILE, 16), TILE), :] = s2[k, t]
 
+    def direct_out(b):
+        return rcopy(acs.at[b], a1.at[t], a1s.at[b], a1r.at[t], along_t(b))
+
+    def direct_back(b):
+        return rcopy(a2.at[b], a3.at[t], a3s.at[b], a3r.at[t], along_t(b))
+
+    def direct_start():
+        @pl.loop(1, NT)
+        def _(o):
+            direct_out((t + o) % NT).start()
+
+        a1[t] = acs[t]
+
+    def unpack_own():
+        for g in get_own:
+            g.wait()
+
+        @pl.loop(0, DIRECT // 64)
+        def _(blk):
+            rows = pl.ds(pl.multiple_of(blk * 64, 64), 64)
+            for k, halves in enumerate(unpacked(dbuf[rows, :])):
+                for c in range(2):
+                    own[k, rows, 128 * c : 128 * c + 128] = halves[c]
+
+    def direct_rotate():
+        @pl.loop(1, NT)
+        def _(o):
+            b = (t + o) % NT
+            rcopy(acs.at[0], a1.at[b], a1s.at[0], a1r.at[b], along_t(b)).wait_recv()
+
+        for cut in range(DIRECT // 128):
+            lanes = slice(128 * cut, 128 * cut + 128)
+            for b, v in enumerate(butterfly([a1[b, :, lanes].astype(F32) for b in range(NT)])):
+                a2[b, :, lanes] = v.astype(BF16)
+
+        @pl.loop(1, NT)
+        def _(o):
+            direct_back((t + o) % NT).start()
+
+        a3[t] = a2[t]
+
+    def swap_direct():
+        return rcopy(aces, acer, asem.at[0], asem.at[1], along_t(sib))
+
+    def direct_product():
+        @pl.loop(1, NT)
+        def _(o):
+            b = (t + o) % NT
+            rcopy(a2.at[0], a3.at[b], a3s.at[0], a3r.at[b], along_t(b)).wait_recv()
+
+        lhs = a3[...].reshape(ROWS, DIRECT)
+        for k in range(CHUNKS):
+            v = jnp.dot(lhs, own[k], preferred_element_type=F32)
+            aces[k] = jnp.where(core == 0, v[:, 128:], v[:, :128]).astype(BF16)
+            pa[k] = jnp.where(core == 0, v[:, :128], v[:, 128:])
+        swap_direct().start()
+
+    lane16 = iota((TILE, 128), 1)
+
+    def put_direct(blk, rows, quarters):
+        for u in range(2):
+            v, w = quarters[2 * u], quarters[2 * u + 1]
+            at = 384 * u
+            acs[blk, :, at : at + 128] = v[:, :128].astype(BF16)
+            acs[blk, :, at + 128 : at + 256] = jnp.where(
+                lane16 < 64, v[:, 128:], pltpu.roll(w[:, 128:], 64, 1)
+            ).astype(BF16)
+            acs[blk, :, at + 256 : at + 384] = w[:, :128].astype(BF16)
+
+    inner(TAKEN, QPAD - TAKEN, put_direct)
+
+    direct_start()
     inr[x] = ins[x]
+    unpack_own()
 
     def assembled(k):
         @pl.loop(0, TILES)
@@ -214,7 +303,10 @@
 
     def hop(k, step, sign, away):
         yy = (y - sign * away + NY) % NY
-        off, n = NEAR if step < 3 else FAR_UP if sign > 0 else FAR_DOWN
+        off, n = 0, SLICE
+        if step == 3:
+            n = FAR[k % 2 if sign > 0 else 1 - k % 2]
+            off = 0 if sign > 0 else SLICE - n
         part = wbuf.at[k, pl.ds(pl.multiple_of(yy * SLICE + off, 16), n)]
         if sign > 0:
             return rcopy(part, part, us.at[k, step], ur.at[k, step], (up, t))
@@ -259,7 +351,7 @@
         for d in (1, 3, 2):
             src = (x + d) % NX
             rcopy(xs.at[k, 0], xr.at[k, src], xss.at[k, 0], xrs.at[k, src], along_x(src)).wait_recv()
-        total = pk[k, x]
+        total = pk[k, x] + pa[k] + acer[k].astype(F32)
         for d in (1, 2, 3):
             total = total + xr[k, (x + d) % NX].astype(F32)
         top, low = total[:HALF], total[HALF:]
@@ -295,13 +387,10 @@
     ring(3, 1)
     ring(2, 2)
     ring(1, 3)
+    direct_rotate()
     for d in (1, 3, 2):
         src = (x + d) % NX
-        for part, (lo, n) in enumerate(PARTS):
-            cut = pl.ds(lo, n)
-            rcopy(
-                ins.at[0, :, cut], inr.at[src, :, cut], iss.at[0, part], irs.at[src, part], along_x(src)
-            ).wait_recv()
+        rcopy(ins.at[0], inr.at[src], iss.at[0], irs.at[src], along_x(src)).wait_recv()
     ring(0, 4)
     partials(0)
     ring(3, 2)
@@ -316,8 +405,10 @@
     reduce_x(2)
     ring(3, 4)
     partials(3)
+    reduce_x(3)
+    direct_product()
+    swap_direct().wait_recv()
     reduce_z(0)
-    reduce_x(3)
 
     for k in range(CHUNKS):
 
@@ -333,9 +424,14 @@
             def _(o):
                 second(k, (t + o) % NT).wait_send()
 
+    @pl.loop(1, NT)
+    def _(o):
+        direct_out((t + o) % NT).wait_send()
+        direct_back((t + o) % NT).wait_send()
+
+    swap_direct().wait_send()
     for d in (1, 2, 3):
-        for part in range(2):
-            spread((x + d) % NX, part).wait_send()
+        spread((x + d) % NX).wait_send()
     for k in range(CHUNKS):
         for s in range(4):
             hop(k, s, 1, s).wait_send()
@@ -379,18 +475,19 @@
     dma = pltpu.SemaphoreType.DMA
     scratch = [
         vmem((ROWS, BLOCK), BF16),
-        vmem((SLICE + 64, COLS), jnp.int32),
+        vmem((SLICE, COLS), jnp.int32),
+        vmem((DIRECT, COLS), jnp.int32),
         vmem((INNER_M, INNER_M), F32),
         vmem((8, 128), jnp.int32),
         vmem((128, 128), F32),
         vmem((QPAD + 64, QPAD), BF16),
-        vmem((4, ROWS, 512), F32),
+        vmem((4, ROWS, TAKEN), F32),
         vmem((CHUNKS, TILES, TILE, COLS), BF16),
         vmem((CHUNKS, NT, TILE, COLS), BF16),
         vmem((CHUNKS, NT, TILE, COLS), BF16),
-        vmem((CHUNKS, QPAD, COLS), BF16),
-        vmem((NX, ROWS, QPAD), BF16),
-        vmem((NX, ROWS, QPAD), BF16),
+        vmem((CHUNKS, TAKEN, COLS), BF16),
+        vmem((NX, ROWS, TAKEN), BF16),
+        vmem((NX, ROWS, TAKEN), BF16),
         vmem((CHUNKS, NX, ROWS, 128), F32),
         vmem((CHUNKS, NX, ROWS, 128), BF16),
         vmem((CHUNKS, NX, ROWS, 128), BF16),
@@ -399,14 +496,23 @@
         vmem((CHUNKS, 2, HALF, 128), BF16),
         vmem((8, HALF, 128), BF16),
         vmem((HALF, 128), F32),
-        dma((4,)),
+        vmem((CHUNKS, DIRECT, COLS), BF16),
+        vmem((NT, TILE, DIRECT), BF16),
+        vmem((NT, TILE, DIRECT), BF16),
+        vmem((NT, TILE, DIRECT), BF16),
+        vmem((NT, TILE, DIRECT), BF16),
+        vmem((CHUNKS, ROWS, 128), F32),
+        vmem((CHUNKS, ROWS, 128), BF16),
+        vmem((CHUNKS, ROWS, 128), BF16),
+        dma((10,)),
         dma((CHUNKS, TILES)), dma((CHUNKS, NT)),
         dma((CHUNKS, NT)), dma((CHUNKS, TILES)),
         dma((CHUNKS, 4)), dma((CHUNKS, 4)), dma((CHUNKS, 4)), dma((CHUNKS, 4)),
-        dma((NX, 2)), dma((NX, 2)),
+        dma((NX,)), dma((NX,)),
         dma((CHUNKS,)), dma((CHUNKS,)),
         dma((CHUNKS, NX)), dma((CHUNKS, NX)),
         dma((CHUNKS, 2)), dma((8,)),
+        dma((NT,)), dma((NT,)), dma((NT,)), dma((NT,)), dma((2,)),
     ]
     in_hbm, in_vmem = pl.BlockSpec(memory_space=pltpu.HBM), pl.BlockSpec(memory_space=pltpu.VMEM)
     return pl.pallas_call(

time: 65.1 us -> 62.9 us (0.966)
  Pallas kernels: 63 us -> 60.9 us
    pallas_call x1, Pallas kernels: 63 us -> 60.9 us  [per_device(): pl.pallas_call(kernel, out_shape=jax.ShapeDtypeStruct((64, ROWS), BF16),...]
where the time goes in v4:
time: 62.9 us; the launch traced here: 62.3 us
  Pallas kernels  60.9 us (97%)
  local copies, waits for them, and re-layouts  1.38 us (2%)
    pallas_call x1, Pallas kernels, per_device(): pl.pallas_call(kernel, out_shape=jax.ShapeDtypeStruct((64, ROWS), BF16),...  60.9 us
    unnamed x1, local copies, waits for them, and re-layouts  1.38 us

profile of v4, /device:TPU:1, one launch (start us, length us, event | category | flops | bytes accessed | tf_op | source)
XLA Modules:
  0.0 62.3 jit_solution(17046008854293532917)
XLA Ops:
  0.0 60.9 %rotated_projection.1 = bf16[64,256]{1,0:T(8,128)(2,1)} custom-call(bf16[256,3328]{1,0:T(8,128)(2,1)} %acts.1, f32[52,52]{1,0:T(8,128)} %mix.1, s32[3328,256]{1,0:T(8,128)} %codes.1, s32[8,128]{1,0:T(8,128)} %bitcast.3), custom_call_target="tpu_custom_call" | custom-call | tf_op jit(solution)/shard_map/rotated_projection/pallas_call | solution.py:518
  60.9 1.4 %copy.6 = bf16[256,64]{0,1:T(8,128)(2,1)} copy(bf16[256,64]{0,1:T(8,128)(2,1)} %bitcast.2) | data formatting | bytes 65536

commit v5 on v4

--- a/solution.py
+++ b/solution.py
@@ -59,6 +59,9 @@
     get_acts = pltpu.make_async_copy(acts, xbuf, lsem.at[1])
     get_mix = pltpu.make_async_copy(mix, mixv, lsem.at[2])
     get_expo = pltpu.make_async_copy(expo, ebuf, lsem.at[3])
+    def all_of(ref, ssem, rsem):
+        return rcopy(ref, ref, ssem, rsem, along_t(sib))
+
     get_own = []
     for u in range(2):
         for at, row, n in (
@@ -144,7 +147,7 @@
         return (TILES * k + i) % NT
 
     def first(k, i):
-        return rcopy(s1.at[k, i], r1.at[k, t], s1s.at[k, i], s1r.at[k, t], along_t(owner(k, i)))
+        return rcopy(s1.at[k, i], r1.at[k, t], s1s.at[k], s1r.at[k], along_t(owner(k, i)))
 
     for k in range(CHUNKS):
 
@@ -159,7 +162,7 @@
     get_acts.wait()
 
     def spread(q):
-        return rcopy(ins.at[q], inr.at[x], iss.at[q], irs.at[x], along_x(q))
+        return rcopy(ins.at[q], inr.at[x], iss, irs, along_x(q))
 
     def inner(lo, n, put):
         for q in range(4):
@@ -190,7 +193,7 @@
 
     def second(k, a):
         i = mine(k)
-        return rcopy(s2.at[k, a], tile_at(k, i), s2s.at[k, a], s2r.at[k, i], along_t(a))
+        return rcopy(s2.at[k, a], tile_at(k, i), s2s.at[k], s2r.at[k], along_t(a))
 
     def butterfly(v):
         for bit in (1, 2, 4, 8):
@@ -201,10 +204,7 @@
 
         @pl.when(mine(k) < TILES)
         def _():
-            @pl.loop(1, NT)
-            def _(o):
-                b = (t + o) % NT
-                rcopy(s1.at[k, 0], r1.at[k, b], s1s.at[k, 0], s1r.at[k, b], along_t(b)).wait_recv()
+            all_of(r1.at[k, pl.ds(0, NT - 1)], s1s.at[k], s1r.at[k]).wait_recv()
 
             i = mine(k)
             r1[k, t] = s1[k, i]
@@ -220,10 +220,10 @@
             wbuf[k, pl.ds(pl.multiple_of(y * SLICE + i * TILE, 16), TILE), :] = s2[k, t]
 
     def direct_out(b):
-        return rcopy(acs.at[b], a1.at[t], a1s.at[b], a1r.at[t], along_t(b))
+        return rcopy(acs.at[b], a1.at[t], a1s, a1r, along_t(b))
 
     def direct_back(b):
-        return rcopy(a2.at[b], a3.at[t], a3s.at[b], a3r.at[t], along_t(b))
+        return rcopy(a2.at[b], a3.at[t], a3s, a3r, along_t(b))
 
     def direct_start():
         @pl.loop(1, NT)
@@ -244,10 +244,7 @@
                     own[k, rows, 128 * c : 128 * c + 128] = halves[c]
 
     def direct_rotate():
-        @pl.loop(1, NT)
-        def _(o):
-            b = (t + o) % NT
-            rcopy(acs.at[0], a1.at[b], a1s.at[0], a1r.at[b], along_t(b)).wait_recv()
+        all_of(a1.at[pl.ds(0, NT - 1)], a1s, a1r).wait_recv()
 
         for cut in range(DIRECT // 128):
             lanes = slice(128 * cut, 128 * cut + 128)
@@ -264,10 +261,7 @@
         return rcopy(aces, acer, asem.at[0], asem.at[1], along_t(sib))
 
     def direct_product():
-        @pl.loop(1, NT)
-        def _(o):
-            b = (t + o) % NT
-            rcopy(a2.at[0], a3.at[b], a3s.at[0], a3r.at[b], along_t(b)).wait_recv()
+        all_of(a3.at[pl.ds(0, NT - 1)], a3s, a3r).wait_recv()
 
         lhs = a3[...].reshape(ROWS, DIRECT)
         for k in range(CHUNKS):
@@ -295,11 +289,15 @@
     unpack_own()
 
     def assembled(k):
-        @pl.loop(0, TILES)
-        def _(i):
-            @pl.when(owner(k, i) != t)
-            def _():
-                rcopy(s2.at[k, 0], tile_at(k, i), s2s.at[k, 0], s2r.at[k, i], along_t(owner(k, i))).wait_recv()
+        here = pl.multiple_of(y * SLICE, 16)
+
+        @pl.when(mine(k) < TILES)
+        def _():
+            all_of(wbuf.at[k, pl.ds(here, SLICE - TILE)], s2s.at[k], s2r.at[k]).wait_recv()
+
+        @pl.when(mine(k) >= TILES)
+        def _():
+            all_of(wbuf.at[k, pl.ds(here, SLICE)], s2s.at[k], s2r.at[k]).wait_recv()
 
     def hop(k, step, sign, away):
         yy = (y - sign * away + NY) % NY
@@ -309,8 +307,8 @@
             off = 0 if sign > 0 else SLICE - n
         part = wbuf.at[k, pl.ds(pl.multiple_of(yy * SLICE + off, 16), n)]
         if sign > 0:
-            return rcopy(part, part, us.at[k, step], ur.at[k, step], (up, t))
-        return rcopy(part, part, ds.at[k, step], dr.at[k, step], (down, t))
+            return rcopy(part, part, us.at[k], ur.at[k, step], (up, t))
+        return rcopy(part, part, ds.at[k], dr.at[k, step], (down, t))
 
     def ring(k, s):
         for sign in (1, -1):
@@ -331,7 +329,7 @@
         swap_cores(k).start()
 
     def over_x(k, p):
-        return rcopy(xs.at[k, p], xr.at[k, x], xss.at[k, p], xrs.at[k, x], along_x(p))
+        return rcopy(xs.at[k, p], xr.at[k, x], xss.at[k], xrs.at[k], along_x(p))
 
     def reduce_x(k):
         swap_cores(k).wait_recv()
@@ -343,14 +341,12 @@
             over_x(k, (x + d) % NX).start()
 
     def over_z(k, i):
-        return rcopy(zs.at[k, i], zr.at[z], zss.at[k, i], zrs.at[z], along_t(2 * (k + 4 * i) + core))
+        return rcopy(zs.at[k, i], zr.at[z], zss.at[k, i], zrs, along_t(2 * (k + 4 * i) + core))
 
     lane1 = iota((HALF, 128), 1)
 
     def reduce_z(k):
-        for d in (1, 3, 2):
-            src = (x + d) % NX
-            rcopy(xs.at[k, 0], xr.at[k, src], xss.at[k, 0], xrs.at[k, src], along_x(src)).wait_recv()
+        all_of(xr.at[k, pl.ds(0, NX - 1)], xss.at[k], xrs.at[k]).wait_recv()
         total = pk[k, x] + pa[k] + acer[k].astype(F32)
         for d in (1, 2, 3):
             total = total + xr[k, (x + d) % NX].astype(F32)
@@ -388,9 +384,7 @@
     ring(2, 2)
     ring(1, 3)
     direct_rotate()
-    for d in (1, 3, 2):
-        src = (x + d) % NX
-        rcopy(ins.at[0], inr.at[src], iss.at[0], irs.at[src], along_x(src)).wait_recv()
+    all_of(inr.at[pl.ds(0, NX - 1)], iss, irs).wait_recv()
     ring(0, 4)
     partials(0)
     ring(3, 2)
@@ -412,38 +406,30 @@
 
     for k in range(CHUNKS):
 
-        @pl.loop(0, TILES)
-        def _(i):
-            @pl.when(owner(k, i) != t)
-            def _():
-                first(k, i).wait_send()
-
         @pl.when(mine(k) < TILES)
         def _():
-            @pl.loop(1, NT)
-            def _(o):
-                second(k, (t + o) % NT).wait_send()
-
-    @pl.loop(1, NT)
-    def _(o):
-        direct_out((t + o) % NT).wait_send()
-        direct_back((t + o) % NT).wait_send()
-
-    swap_direct().wait_send()
-    for d in (1, 2, 3):
-        spread((x + d) % NX).wait_send()
-    for k in range(CHUNKS):
-        for s in range(4):
-            hop(k, s, 1, s).wait_send()
-            hop(k, s, -1, s).wait_send()
+            all_of(s1.at[k, pl.ds(0, TILES - 1)], s1s.at[k], s1r.at[k]).wait_send()
+            all_of(s2.at[k, pl.ds(0, NT - 1)], s2s.at[k], s2r.at[k]).wait_send()
+
+        @pl.when(mine(k) >= TILES)
+        def _():
+            all_of(s1.at[k], s1s.at[k], s1r.at[k]).wait_send()
+
+        for sign, (ssem, rsem) in ((1, (us, ur)), (-1, (ds, dr))):
+            n = 3 * SLICE + FAR[k % 2 if sign > 0 else 1 - k % 2]
+            all_of(wbuf.at[k, pl.ds(0, n)], ssem.at[k], rsem.at[k, 0]).wait_send()
         swap_cores(k).wait_send()
+
+    all_of(acs.at[pl.ds(0, NT - 1)], a1s, a1r).wait_send()
+    all_of(ins.at[pl.ds(0, NX - 1)], iss, irs).wait_send()
 
     reduce_z(1)
     reduce_z(2)
     reduce_z(3)
+    all_of(a2.at[pl.ds(0, NT - 1)], a3s, a3r).wait_send()
+    swap_direct().wait_send()
     for k in range(CHUNKS):
-        for d in (1, 2, 3):
-            over_x(k, (x + d) % NX).wait_send()
+        all_of(xs.at[k, pl.ds(0, NX - 1)], xss.at[k], xrs.at[k]).wait_send()
 
     get_expo.wait()
     lane8 = iota((8, 128), 1)
@@ -452,12 +438,8 @@
         (lane8 < 64) == (core == 0), jnp.left_shift(1, e + 16), jnp.left_shift(1, pltpu.roll(e, 64, 1) + 16)
     ).astype(F32)
 
-    def total_of_z(o, acc):
-        src = (z + o) % 8
-        rcopy(zs.at[0, 0], zr.at[src], zss.at[0, 0], zrs.at[src], along_t(2 * src + core)).wait_recv()
-        return acc + zr[src].astype(F32)
-
-    total = lax.fori_loop(1, 8, total_of_z, fs[...])
+    all_of(zr.at[pl.ds(0, 7)], zss.at[0, 0], zrs).wait_recv()
+    total = lax.fori_loop(1, 8, lambda o, acc: acc + zr[(z + o) % 8].astype(F32), fs[...])
     total = total * (mpad[pl.ds(z, 1), :] * (2.0 ** -28))
     turned = total.T
     out[:, 0:HALF] = turned[0:64].astype(BF16)
@@ -505,14 +487,14 @@
         vmem((CHUNKS, ROWS, 128), BF16),
         vmem((CHUNKS, ROWS, 128), BF16),
         dma((10,)),
-        dma((CHUNKS, TILES)), dma((CHUNKS, NT)),
-        dma((CHUNKS, NT)), dma((CHUNKS, TILES)),
-        dma((CHUNKS, 4)), dma((CHUNKS, 4)), dma((CHUNKS, 4)), dma((CHUNKS, 4)),
-        dma((NX,)), dma((NX,)),
         dma((CHUNKS,)), dma((CHUNKS,)),
-        dma((CHUNKS, NX)), dma((CHUNKS, NX)),
-        dma((CHUNKS, 2)), dma((8,)),
-        dma((NT,)), dma((NT,)), dma((NT,)), dma((NT,)), dma((2,)),
+        dma((CHUNKS,)), dma((CHUNKS,)),
+        dma((CHUNKS,)), dma((CHUNKS, 4)), dma((CHUNKS,)), dma((CHUNKS, 4)),
+        dma(()), dma(()),
+        dma((CHUNKS,)), dma((CHUNKS,)),
+        dma((CHUNKS,)), dma((CHUNKS,)),
+        dma((CHUNKS, 2)), dma(()),
+        dma(()), dma(()), dma(()), dma(()), dma((2,)),
     ]
     in_hbm, in_vmem = pl.BlockSpec(memory_space=pltpu.HBM), pl.BlockSpec(memory_space=pltpu.VMEM)
     return pl.pallas_call(

time: 62.9 us -> 61.3 us (0.975)
  Pallas kernels: 60.9 us -> 59.8 us
    pallas_call x1, Pallas kernels: 60.9 us -> 59.8 us  [per_device(): pl.pallas_call(kernel, out_shape=jax.ShapeDtypeStruct((64, ROWS), BF16),...]
where the time goes in v5:
time: 61.3 us; the launch traced here: 61.1 us
  Pallas kernels  59.8 us (98%)
  local copies, waits for them, and re-layouts  1.38 us (2%)
    pallas_call x1, Pallas kernels, per_device(): pl.pallas_call(kernel, out_shape=jax.ShapeDtypeStruct((64, ROWS), BF16),...  59.8 us
    unnamed x1, local copies, waits for them, and re-layouts  1.38 us

profile of v5, /device:TPU:1, one launch (start us, length us, event | category | flops | bytes accessed | tf_op | source)
XLA Modules:
  0.0 61.1 jit_solution(15508356759795965868)
XLA Ops:
  0.0 59.8 %rotated_projection.1 = bf16[64,256]{1,0:T(8,128)(2,1)} custom-call(bf16[256,3328]{1,0:T(8,128)(2,1)} %acts.1, f32[52,52]{1,0:T(8,128)} %mix.1, s32[3328,256]{1,0:T(8,128)} %codes.1, s32[8,128]{1,0:T(8,128)} %bitcast.3), custom_call_target="tpu_custom_call" | custom-call | tf_op jit(solution)/shard_map/rotated_projection/pallas_call | solution.py:500
  59.8 1.4 %copy.6 = bf16[256,64]{0,1:T(8,128)(2,1)} copy(bf16[256,64]{0,1:T(8,128)(2,1)} %bitcast.2) | data formatting | bytes 65536

commit v6 on v5

--- a/solution.py
+++ b/solution.py
@@ -372,32 +372,32 @@
     ring(1, 0)
     assembled(2)
     ring(2, 0)
+    assembled(3)
+    ring(3, 0)
     ring(0, 1)
     ring(1, 1)
-    assembled(3)
-    ring(3, 0)
+    ring(2, 1)
     ring(0, 2)
-    ring(2, 1)
+    ring(3, 1)
     ring(1, 2)
+    ring(2, 2)
     ring(0, 3)
-    ring(3, 1)
-    ring(2, 2)
+    ring(3, 2)
     ring(1, 3)
+    ring(2, 3)
     direct_rotate()
     all_of(inr.at[pl.ds(0, NX - 1)], iss, irs).wait_recv()
     ring(0, 4)
     partials(0)
-    ring(3, 2)
+    ring(3, 3)
     reduce_x(0)
-    ring(2, 3)
     ring(1, 4)
     partials(1)
-    ring(3, 3)
+    ring(2, 4)
     reduce_x(1)
-    ring(2, 4)
     partials(2)
+    ring(3, 4)
     reduce_x(2)
-    ring(3, 4)
     partials(3)
     reduce_x(3)
     direct_product()

time: 61.3 us -> 60.8 us (level)
  no operation moved by 1% of the time
where the time goes in v6:
time: 60.8 us; the launch traced here: 60.6 us
  Pallas kernels  59.3 us (98%)
  local copies, waits for them, and re-layouts  1.38 us (2%)
    pallas_call x1, Pallas kernels, per_device(): pl.pallas_call(kernel, out_shape=jax.ShapeDtypeStruct((64, ROWS), BF16),...  59.3 us
    unnamed x1, local copies, waits for them, and re-layouts  1.38 us

profile of v6, /device:TPU:1, one launch (start us, length us, event | category | flops | bytes accessed | tf_op | source)
XLA Modules:
  0.0 60.6 jit_solution(7198228091864238651)
XLA Ops:
  0.0 59.3 %rotated_projection.1 = bf16[64,256]{1,0:T(8,128)(2,1)} custom-call(bf16[256,3328]{1,0:T(8,128)(2,1)} %acts.1, f32[52,52]{1,0:T(8,128)} %mix.1, s32[3328,256]{1,0:T(8,128)} %codes.1, s32[8,128]{1,0:T(8,128)} %bitcast.3), custom_call_target="tpu_custom_call" | custom-call | tf_op jit(solution)/shard_map/rotated_projection/pallas_call | solution.py:500
  59.3 1.4 %copy.6 = bf16[256,64]{0,1:T(8,128)(2,1)} copy(bf16[256,64]{0,1:T(8,128)(2,1)} %bitcast.2) | data formatting | bytes 65536
